TPU v7x, 512 devices: a whole 4x4x16 slice. The times are simulated.
512 devices in a mesh: tensor: 16 (over y, x), context: 32 (over z, core).
Axes of the slice: x: 4, y: 4, z: 16, core: 2. Of those that a mesh axis runs over, the one named last changes fastest.
Arguments:
- hidden: bfloat16 [8192, 2048], P('context', 'tensor'), may hold values from -6 to 6
- proj_qkvz: bfloat16 [2048, 12288], P(None, 'tensor'), may hold values from -0.125 to 0.125
- proj_rates: bfloat16 [2048, 64], P(None, 'tensor'), may hold values from -0.125 to 0.125
- conv_weight: float32 [4, 16, 512], P(None, 'tensor'), may hold values from -3 to 3
- decay_rate: float32 [32], P('tensor'), may hold values from 1e-05 to 0.1
- step_bias: float32 [32], P('tensor'), may hold values from -1 to 1
- norm_gain: float32 [128], replicated, may hold values from 0.5 to 1.5
- proj_out: bfloat16 [4096, 2048], P('tensor'), may hold values from -0.09375 to 0.09375
- doc_lengths: int32 [8], replicated, may hold values from 1 to 4096, 8192 in all
Outputs:
- layer_out: bfloat16 [8192, 2048], P('context', 'tensor')
Inputs may be any that keep to these rules, and one draw needn't show every extreme that they name: `doc_lengths`: the lengths sum to 8192; the longest is exactly 4096.
All inputs are finite; a program needn't handle non-finite values.
Results may differ from a plain program's by a relative error of at most 0.02.
Values may be sent and summed in bfloat16 or wider, within the bound.
No kernel may reach another device: no remote copies, remote signals or barrier semaphores. Data moves between devices by JAX's collectives and lax.ppermute only.
A program may use at most 64 MiB of HBM per device.

v0:
```python
import math

import jax
import jax.numpy as jnp
from jax import lax
from jax.sharding import PartitionSpec as P

KERNEL = 4
SPAN = 64


PRECISE = lax.Precision.HIGHEST


def from_behind(array, axis, by):
    peers = lax.axis_size(axis)
    pairs = [(i, i + by) for i in range(peers) if 0 <= i + by < peers]
    return lax.ppermute(array, axis, pairs)


def doc_index(positions, bounds):
    return jnp.sum((bounds[None, :] <= positions[:, None]).astype(jnp.int32), axis=1)


def advance(totals, pieces):
    total_map, total_add = totals
    transition, injection = pieces
    new_map = jnp.einsum("hab,hbc->hac", total_map, transition, precision=PRECISE)
    new_add = jnp.einsum("hvk,hkc->hvc", total_add, transition, precision=PRECISE) + injection
    return (new_map, new_add)


def emit_rows(query_blk, gamma_blk, scores_blk, fresh_blk, carried_blk, state_mat):
    direct = gamma_blk[..., None] * jnp.einsum(
        "htk,hvk->htv", query_blk, state_mat, precision=PRECISE
    )
    corrected = fresh_blk - jnp.einsum("hik,hvk->hiv", carried_blk, state_mat, precision=PRECISE)
    return direct + jnp.einsum("hti,hiv->htv", scores_blk, corrected, precision=PRECISE)


def incoming_state(dev_map, dev_add, start_add):

    def relay_step(step_index, state_mat):
        passed = jnp.einsum("hvk,hkc->hvc", state_mat, dev_map, precision=PRECISE) + dev_add
        return from_behind(passed.astype(jnp.bfloat16), "context", 1).astype(passed.dtype)

    return lax.fori_loop(0, lax.axis_size("context") - 1, relay_step, start_add)


def local(
    hidden,
    proj_qkvz,
    proj_rates,
    conv_weight,
    decay_rate,
    step_bias,
    norm_gain,
    proj_out,
    doc_lengths,
):
    tok_rows = hidden.shape[0]
    head_dim = norm_gain.shape[0]
    groups = proj_qkvz.shape[1] // (6 * head_dim)
    head_count = 2 * groups
    blocks = tok_rows // SPAN
    first_row = lax.axis_index("context") * tok_rows
    shard_piece = lax.all_gather(hidden, "tensor", axis=1, tiled=True)
    projected = jnp.dot(shard_piece, proj_qkvz, preferred_element_type=jnp.float32)
    gating = jnp.dot(shard_piece, proj_rates, preferred_element_type=jnp.float32)
    mixed = projected.astype(jnp.bfloat16).reshape(tok_rows, groups, 6 * head_dim)
    rates = gating.astype(jnp.bfloat16).reshape(tok_rows, groups, 4).astype(jnp.float32)
    before = mixed[:, :, : 4 * head_dim]
    rim_rows = from_behind(before[tok_rows - (KERNEL - 1) :], "context", 1)
    extended = jnp.concatenate([rim_rows, before], axis=0).astype(jnp.float32)
    bounds = jnp.cumsum(doc_lengths)[:-1]
    positions = first_row + jnp.arange(tok_rows, dtype=jnp.int32)
    doc_ids = doc_index(positions, bounds)
    convolved = jnp.zeros((tok_rows, groups, 4 * head_dim), jnp.float32)
    for offset in range(KERNEL):
        leading = KERNEL - 1 - offset
        keep_tap = (doc_index(positions - offset, bounds) == doc_ids).astype(jnp.float32)
        convolved = (
            convolved
            + conv_weight[offset][None]
            * extended[leading : leading + tok_rows]
            * keep_tap[:, None, None]
        )
    convolved = jax.nn.silu(convolved)
    query_vecs = convolved[:, :, :head_dim]
    key_vecs = convolved[:, :, head_dim : 2 * head_dim]
    value_vecs = convolved[:, :, 2 * head_dim :].reshape(tok_rows, head_count, head_dim)
    query_vecs = (
        query_vecs
        / jnp.sqrt(jnp.sum(query_vecs * query_vecs, -1, keepdims=True) + 1e-06)
        / math.sqrt(head_dim)
    )
    key_vecs = key_vecs / jnp.sqrt(jnp.sum(key_vecs * key_vecs, -1, keepdims=True) + 1e-06)
    beta_gate = jax.nn.sigmoid(rates[:, :, :2].reshape(tok_rows, head_count))
    decays = -decay_rate[None] * jax.nn.softplus(
        rates[:, :, 2:].reshape(tok_rows, head_count) + step_bias[None]
    )

    def spanned(matrix):
        return matrix.reshape(blocks, SPAN, head_count, head_dim).transpose(0, 2, 1, 3)

    query_blk = spanned(jnp.repeat(query_vecs, 2, axis=1))
    key_blk = spanned(jnp.repeat(key_vecs, 2, axis=1))
    value_blk = spanned(value_vecs)
    beta_blk = beta_gate.reshape(blocks, SPAN, head_count).transpose(0, 2, 1)
    decay_blk = decays.reshape(blocks, SPAN, head_count).transpose(0, 2, 1)
    doc_blk = doc_ids.reshape(blocks, SPAN)
    block_starts = first_row + jnp.arange(blocks, dtype=jnp.int32) * SPAN
    prior_doc = doc_index(block_starts - 1, bounds)
    cumul = jnp.cumsum(decay_blk, axis=2)
    span_eye = jnp.eye(SPAN, dtype=jnp.float32)
    head_eye = jnp.eye(head_dim, dtype=jnp.float32)
    lower_tri = jnp.tril(jnp.ones((SPAN, SPAN), jnp.bool_))
    same_doc = (lower_tri[None] & (doc_blk[:, :, None] == doc_blk[:, None, :]))[:, None]
    differ = cumul[..., :, None] - cumul[..., None, :]
    ratios = jnp.exp(jnp.where(same_doc, differ, 0.0)) * same_doc.astype(jnp.float32)
    gammas = jnp.exp(cumul) * (doc_blk == prior_doc[:, None]).astype(jnp.float32)[:, None]
    tail_ratio = ratios[..., -1, :]
    key_gram = jnp.einsum("chtd,chid->chti", key_blk, key_blk, precision=PRECISE)
    system = span_eye + beta_blk[..., None] * ratios * (1.0 - span_eye) * key_gram
    fresh_rows = jax.scipy.linalg.solve_triangular(
        system, beta_blk[..., None] * value_blk, lower=True, unit_diagonal=True
    )
    carried = jax.scipy.linalg.solve_triangular(
        system, (beta_blk * gammas)[..., None] * key_blk, lower=True, unit_diagonal=True
    )
    scores = jnp.einsum("chtd,chid->chti", query_blk, key_blk, precision=PRECISE) * ratios
    transition = gammas[..., -1][..., None, None] * head_eye - jnp.einsum(
        "chia,chi,chib->chab", carried, tail_ratio, key_blk, precision=PRECISE
    )
    injection = jnp.einsum(
        "chiv,chi,chik->chvk", fresh_rows, tail_ratio, key_blk, precision=PRECISE
    )
    start_map = jnp.broadcast_to(head_eye, (head_count, head_dim, head_dim))
    start_add = jnp.zeros((head_count, head_dim, head_dim), jnp.float32)
    pieces = (query_blk, gammas, scores, fresh_rows, carried, transition, injection)

    def compose_fn(totals, piece_pair):
        return (advance(totals, piece_pair), None)

    (dev_map, dev_add), _ = lax.scan(compose_fn, (start_map, start_add), (transition, injection))
    entering = incoming_state(dev_map, dev_add, start_add)

    def replay_fn(state_mat, piece_set):
        query_one, gamma_one, scores_one, fresh_one, carried_one, trans_one, inject_one = piece_set
        emitted = emit_rows(query_one, gamma_one, scores_one, fresh_one, carried_one, state_mat)
        next_state = (
            jnp.einsum("hvk,hkc->hvc", state_mat, trans_one, precision=PRECISE) + inject_one
        )
        return (next_state, emitted)

    _, outputs = lax.scan(replay_fn, entering, pieces)
    outputs = outputs.transpose(0, 2, 1, 3).reshape(tok_rows, head_count, head_dim)
    out_gate = (
        mixed[:, :, 4 * head_dim :].reshape(tok_rows, head_count, head_dim).astype(jnp.float32)
    )
    rms_scale = lax.rsqrt(jnp.mean(outputs * outputs, -1, keepdims=True) + 1e-06)
    normed = (outputs * rms_scale * norm_gain * jax.nn.silu(out_gate)).astype(jnp.bfloat16)
    normed = normed.reshape(tok_rows, head_count * head_dim)
    partial_sum = jnp.dot(normed, proj_out, preferred_element_type=jnp.float32)
    return lax.psum_scatter(
        partial_sum.astype(jnp.bfloat16), "tensor", scatter_dimension=1, tiled=True
    )


def solution(mesh):
    placed = (
        P("context", "tensor"),
        P(None, "tensor"),
        P(None, "tensor"),
        P(None, "tensor", None),
        P("tensor"),
        P("tensor"),
        P(),
        P("tensor", None),
        P(),
    )
    return jax.shard_map(
        local, mesh=mesh, in_specs=placed, out_specs=P("context", "tensor"), check_vma=False
    )
```

profile of v0, /device:TPU:2, one launch (start us, length us, event | category | flops | bytes accessed | tf_op | source)
XLA Modules:
  0.0 531.5 jit_solution(13012258134882855134)
XLA Ops:
  17.0 56.1 %all-gather.2.cloned.1.call-done = bf16[256,2048]{1,0:T(8,128)(2,1)} async-done(((bf16[256,128]{1,0:T(8,128)(2,1)}), bf16[256,2048]{1,0:T(8,128)(2,1)}) %all-gather.2.cloned.1.call-update) | async-done | bytes 1048592 | tf_op jit(solution)/shard_map/all_gather | solution.py:67
  90.2 40.7 %custom-call.6 = f32[4,2,1,64,64]{3,4,2,1,0:T(8,128)} custom-call(f32[4,2,1,64,64]{4,3,2,1,0:T(8,128)} %fusion.36), custom_call_target="InvertDiagBlocksLowerTriangular" | custom-call | tf_op jit(solution)/shard_map/jit(_solve_triangular)/vmap(vmap())/triangular_solve | solution.py:128
  143.6 9.9 %while.37 = (s32[]{:T(128)}, f32[2,128,128]{1,2,0:T(8,128)S(1)}, f32[2,128,128]{1,2,0:T(8,128)S(1)}, f32[4,2,128,128]{2,3,1,0:T(8,128)}, f32[4,2,128,128]{2,3,1,0:T(8,128)}, /*index=5*/s32[]{:T(128)}, s32[]{:T(128)}) while((s32[]{:T(128)}, f32[2,128,128]{1,2,0:T(8,128)S(1)}, f32[2,128,128]{1,2,0:T(8,128)S(1)}, ...), condition=%wide.region_9.11_spmd.clone, body=%wide.region_8.10_spmd.clone.sunk | while | flops 100728832 | bytes 1443415 | solution.py:145
  154.4 226.0 %while.38 = (s32[]{:T(128)}, f32[2,128,128]{2,1,0:T(8,128)S(1)}, f32[2,128,128]{2,1,0:T(8,128)}, f32[2,128,128]{2,1,0:T(8,128)S(1)}, s32[]{:T(128)}, /*index=5*/s32[]{:T(128)}) while((s32[]{:T(128)}, f32[2,128,128]{2,1,0:T(8,128)S(1)}, f32[2,128,128]{2,1,0:T(8,128)}, f32[2,128,128]{2,1,0:T(8,128)S(1)}, s32[]{:T(128)}, ...), condition=%wide.region_11.13_spmd.clone, body=%wide.region_10.12_spmd.clone.sunk | while | flops 50462720 | bytes 917623 | solution.py:47
  165.8 4.7 collective-permute-start
  172.6 4.7 collective-permute-start
  179.4 4.7 collective-permute-start
  186.2 4.7 collective-permute-start
  193.0 4.7 collective-permute-start
  199.8 4.7 collective-permute-start
  206.6 4.7 collective-permute-start
  220.2 4.7 collective-permute-start
  233.8 4.7 collective-permute-start
  247.4 4.7 collective-permute-start
  254.2 5.2 collective-permute-start
  261.5 5.9 %collective-permute-start = (bf16[2,128,128]{2,1,0:T(8,128)(2,1)S(1)}, bf16[2,128,128]{2,1,0:T(8,128)(2,1)S(1)}, u32[]{:S(2)}, u32[]{:S(2)}) collective-permute-start(bf16[2,128,128]{2,1,0:T(8,128)(2,1)S(1)} %fusion.140), channel_id=1, source_target_pairs={{0,1},{1,2},{2,3},{3,4},{4,5},{5,6},{6,7},{7,8},{8,9},{9,10},{10,1... | collective-permute-start | bytes 196616 | tf_op jit(solution)/shard_map/while/body/eval_jaxpr/ppermute | solution.py:18
  269.5 5.9 %collective-permute-start = (bf16[2,128,128]{2,1,0:T(8,128)(2,1)S(1)}, bf16[2,128,128]{2,1,0:T(8,128)(2,1)S(1)}, u32[]{:S(2)}, u32[]{:S(2)}) collective-permute-start(bf16[2,128,128]{2,1,0:T(8,128)(2,1)S(1)} %fusion.140), channel_id=1, source_target_pairs={{0,1},{1,2},{2,3},{3,4},{4,5},{5,6},{6,7},{7,8},{8,9},{9,10},{10,1... | collective-permute-start | bytes 196616 | tf_op jit(solution)/shard_map/while/body/eval_jaxpr/ppermute | solution.py:18
  277.5 5.9 %collective-permute-start = (bf16[2,128,128]{2,1,0:T(8,128)(2,1)S(1)}, bf16[2,128,128]{2,1,0:T(8,128)(2,1)S(1)}, u32[]{:S(2)}, u32[]{:S(2)}) collective-permute-start(bf16[2,128,128]{2,1,0:T(8,128)(2,1)S(1)} %fusion.140), channel_id=1, source_target_pairs={{0,1},{1,2},{2,3},{3,4},{4,5},{5,6},{6,7},{7,8},{8,9},{9,10},{10,1... | collective-permute-start | bytes 196616 | tf_op jit(solution)/shard_map/while/body/eval_jaxpr/ppermute | solution.py:18
  285.5 5.9 %collective-permute-start = (bf16[2,128,128]{2,1,0:T(8,128)(2,1)S(1)}, bf16[2,128,128]{2,1,0:T(8,128)(2,1)S(1)}, u32[]{:S(2)}, u32[]{:S(2)}) collective-permute-start(bf16[2,128,128]{2,1,0:T(8,128)(2,1)S(1)} %fusion.140), channel_id=1, source_target_pairs={{0,1},{1,2},{2,3},{3,4},{4,5},{5,6},{6,7},{7,8},{8,9},{9,10},{10,1... | collective-permute-start | bytes 196616 | tf_op jit(solution)/shard_map/while/body/eval_jaxpr/ppermute | solution.py:18
  293.5 5.9 %collective-permute-start = (bf16[2,128,128]{2,1,0:T(8,128)(2,1)S(1)}, bf16[2,128,128]{2,1,0:T(8,128)(2,1)S(1)}, u32[]{:S(2)}, u32[]{:S(2)}) collective-permute-start(bf16[2,128,128]{2,1,0:T(8,128)(2,1)S(1)} %fusion.140), channel_id=1, source_target_pairs={{0,1},{1,2},{2,3},{3,4},{4,5},{5,6},{6,7},{7,8},{8,9},{9,10},{10,1... | collective-permute-start | bytes 196616 | tf_op jit(solution)/shard_map/while/body/eval_jaxpr/ppermute | solution.py:18
  301.5 5.9 %collective-permute-start = (bf16[2,128,128]{2,1,0:T(8,128)(2,1)S(1)}, bf16[2,128,128]{2,1,0:T(8,128)(2,1)S(1)}, u32[]{:S(2)}, u32[]{:S(2)}) collective-permute-start(bf16[2,128,128]{2,1,0:T(8,128)(2,1)S(1)} %fusion.140), channel_id=1, source_target_pairs={{0,1},{1,2},{2,3},{3,4},{4,5},{5,6},{6,7},{7,8},{8,9},{9,10},{10,1... | collective-permute-start | bytes 196616 | tf_op jit(solution)/shard_map/while/body/eval_jaxpr/ppermute | solution.py:18
  309.5 5.9 %collective-permute-start = (bf16[2,128,128]{2,1,0:T(8,128)(2,1)S(1)}, bf16[2,128,128]{2,1,0:T(8,128)(2,1)S(1)}, u32[]{:S(2)}, u32[]{:S(2)}) collective-permute-start(bf16[2,128,128]{2,1,0:T(8,128)(2,1)S(1)} %fusion.140), channel_id=1, source_target_pairs={{0,1},{1,2},{2,3},{3,4},{4,5},{5,6},{6,7},{7,8},{8,9},{9,10},{10,1... | collective-permute-start | bytes 196616 | tf_op jit(solution)/shard_map/while/body/eval_jaxpr/ppermute | solution.py:18
  317.5 5.9 %collective-permute-start = (bf16[2,128,128]{2,1,0:T(8,128)(2,1)S(1)}, bf16[2,128,128]{2,1,0:T(8,128)(2,1)S(1)}, u32[]{:S(2)}, u32[]{:S(2)}) collective-permute-start(bf16[2,128,128]{2,1,0:T(8,128)(2,1)S(1)} %fusion.140), channel_id=1, source_target_pairs={{0,1},{1,2},{2,3},{3,4},{4,5},{5,6},{6,7},{7,8},{8,9},{9,10},{10,1... | collective-permute-start | bytes 196616 | tf_op jit(solution)/shard_map/while/body/eval_jaxpr/ppermute | solution.py:18
  325.5 5.9 %collective-permute-start = (bf16[2,128,128]{2,1,0:T(8,128)(2,1)S(1)}, bf16[2,128,128]{2,1,0:T(8,128)(2,1)S(1)}, u32[]{:S(2)}, u32[]{:S(2)}) collective-permute-start(bf16[2,128,128]{2,1,0:T(8,128)(2,1)S(1)} %fusion.140), channel_id=1, source_target_pairs={{0,1},{1,2},{2,3},{3,4},{4,5},{5,6},{6,7},{7,8},{8,9},{9,10},{10,1... | collective-permute-start | bytes 196616 | tf_op jit(solution)/shard_map/while/body/eval_jaxpr/ppermute | solution.py:18
  333.5 5.9 %collective-permute-start = (bf16[2,128,128]{2,1,0:T(8,128)(2,1)S(1)}, bf16[2,128,128]{2,1,0:T(8,128)(2,1)S(1)}, u32[]{:S(2)}, u32[]{:S(2)}) collective-permute-start(bf16[2,128,128]{2,1,0:T(8,128)(2,1)S(1)} %fusion.140), channel_id=1, source_target_pairs={{0,1},{1,2},{2,3},{3,4},{4,5},{5,6},{6,7},{7,8},{8,9},{9,10},{10,1... | collective-permute-start | bytes 196616 | tf_op jit(solution)/shard_map/while/body/eval_jaxpr/ppermute | solution.py:18
  341.6 5.9 %collective-permute-start = (bf16[2,128,128]{2,1,0:T(8,128)(2,1)S(1)}, bf16[2,128,128]{2,1,0:T(8,128)(2,1)S(1)}, u32[]{:S(2)}, u32[]{:S(2)}) collective-permute-start(bf16[2,128,128]{2,1,0:T(8,128)(2,1)S(1)} %fusion.140), channel_id=1, source_target_pairs={{0,1},{1,2},{2,3},{3,4},{4,5},{5,6},{6,7},{7,8},{8,9},{9,10},{10,1... | collective-permute-start | bytes 196616 | tf_op jit(solution)/shard_map/while/body/eval_jaxpr/ppermute | solution.py:18
  349.6 5.9 %collective-permute-start = (bf16[2,128,128]{2,1,0:T(8,128)(2,1)S(1)}, bf16[2,128,128]{2,1,0:T(8,128)(2,1)S(1)}, u32[]{:S(2)}, u32[]{:S(2)}) collective-permute-start(bf16[2,128,128]{2,1,0:T(8,128)(2,1)S(1)} %fusion.140), channel_id=1, source_target_pairs={{0,1},{1,2},{2,3},{3,4},{4,5},{5,6},{6,7},{7,8},{8,9},{9,10},{10,1... | collective-permute-start | bytes 196616 | tf_op jit(solution)/shard_map/while/body/eval_jaxpr/ppermute | solution.py:18
  357.6 5.9 %collective-permute-start = (bf16[2,128,128]{2,1,0:T(8,128)(2,1)S(1)}, bf16[2,128,128]{2,1,0:T(8,128)(2,1)S(1)}, u32[]{:S(2)}, u32[]{:S(2)}) collective-permute-start(bf16[2,128,128]{2,1,0:T(8,128)(2,1)S(1)} %fusion.140), channel_id=1, source_target_pairs={{0,1},{1,2},{2,3},{3,4},{4,5},{5,6},{6,7},{7,8},{8,9},{9,10},{10,1... | collective-permute-start | bytes 196616 | tf_op jit(solution)/shard_map/while/body/eval_jaxpr/ppermute | solution.py:18
  365.6 5.9 %collective-permute-start = (bf16[2,128,128]{2,1,0:T(8,128)(2,1)S(1)}, bf16[2,128,128]{2,1,0:T(8,128)(2,1)S(1)}, u32[]{:S(2)}, u32[]{:S(2)}) collective-permute-start(bf16[2,128,128]{2,1,0:T(8,128)(2,1)S(1)} %fusion.140), channel_id=1, source_target_pairs={{0,1},{1,2},{2,3},{3,4},{4,5},{5,6},{6,7},{7,8},{8,9},{9,10},{10,1... | collective-permute-start | bytes 196616 | tf_op jit(solution)/shard_map/while/body/eval_jaxpr/ppermute | solution.py:18
  373.6 5.9 %collective-permute-start = (bf16[2,128,128]{2,1,0:T(8,128)(2,1)S(1)}, bf16[2,128,128]{2,1,0:T(8,128)(2,1)S(1)}, u32[]{:S(2)}, u32[]{:S(2)}) collective-permute-start(bf16[2,128,128]{2,1,0:T(8,128)(2,1)S(1)} %fusion.140), channel_id=1, source_target_pairs={{0,1},{1,2},{2,3},{3,4},{4,5},{5,6},{6,7},{7,8},{8,9},{9,10},{10,1... | collective-permute-start | bytes 196616 | tf_op jit(solution)/shard_map/while/body/eval_jaxpr/ppermute | solution.py:18
  384.4 20.6 %while.36 = (s32[]{:T(128)}, f32[2,128,128]{1,2,0:T(8,128)S(1)}, f32[4,2,64,128]{3,2,1,0:T(8,128)}, f32[4,2,128,128]{2,3,1,0:T(8,128)}, f32[4,2,128,128]{2,3,1,0...) while((s32[]{:T(128)}, f32[2,128,128]{1,2,0:T(8,128)S(1)}, ...), condition=%wide.region_14.16_spmd, body=%wide.region_13.15_spmd.sunk | while | flops 113328128 | bytes 1643633 | solution.py:156
  412.8 110.3 %reduce-scatter.4.cloned.1.call-done = bf16[128,256]{1,0:T(8,128)(2,1)} async-done(((bf16[2048,256]{1,0:T(8,128)(2,1)}), bf16[128,256]{1,0:T(8,128)(2,1)}) %reduce-scatter.4.cloned.1.call-update) | async-done | bytes 65552
  (244 shorter events, 168.5 us)
Async XLA Ops:
  6.5 66.6 %all-gather.2.cloned.1.call-start = ((), (), s32[]{:S(2)}) async-start(), calls=%async_computation.1 | async-start | bytes 1114112 | tf_op jit(solution)/shard_map/all_gather | solution.py:67
  7.3 515.8 %reduce-scatter.4.cloned.1.call-start = ((), (), s32[]{:S(2)}) async-start(), calls=%async_computation.2 | async-start | bytes 1114112
  76.1 8.9 %collective-permute-start.1 = (bf16[3,1,512]{2,0,1:T(4,128)(2,1)}, bf16[3,1,512]{2,0,1:T(4,128)(2,1)}, u32[]{:S(2)}, u32[]{:S(2)}) collective-permute-start(bf16[3,1,512]{2,0,1:T(4,128)(2,1)} %slice.85), channel_id=1, source_target_pairs={{0,1},{1,2},{2,3},{3,4},{4,5},{5,6},{6,7},{7,8},{8,9},{9,10},{10,1... | collective-permute-start | bytes 9224 | tf_op jit(solution)/shard_map/ppermute | solution.py:18
  165.8 5.6 %collective-permute-start = (bf16[2,128,128]{2,1,0:T(8,128)(2,1)S(1)}, bf16[2,128,128]{2,1,0:T(8,128)(2,1)S(1)}, u32[]{:S(2)}, u32[]{:S(2)}) collective-permute-start(bf16[2,128,128]{2,1,0:T(8,128)(2,1)S(1)} %fusion.140), channel_id=1, source_target_pairs={{0,1},{1,2},{2,3},{3,4},{4,5},{5,6},{6,7},{7,8},{8,9},{9,10},{10,1... | collective-permute-start | bytes 196616 | tf_op jit(solution)/shard_map/while/body/eval_jaxpr/ppermute | solution.py:18
  172.6 5.6 %collective-permute-start = (bf16[2,128,128]{2,1,0:T(8,128)(2,1)S(1)}, bf16[2,128,128]{2,1,0:T(8,128)(2,1)S(1)}, u32[]{:S(2)}, u32[]{:S(2)}) collective-permute-start(bf16[2,128,128]{2,1,0:T(8,128)(2,1)S(1)} %fusion.140), channel_id=1, source_target_pairs={{0,1},{1,2},{2,3},{3,4},{4,5},{5,6},{6,7},{7,8},{8,9},{9,10},{10,1... | collective-permute-start | bytes 196616 | tf_op jit(solution)/shard_map/while/body/eval_jaxpr/ppermute | solution.py:18
  179.4 5.6 %collective-permute-start = (bf16[2,128,128]{2,1,0:T(8,128)(2,1)S(1)}, bf16[2,128,128]{2,1,0:T(8,128)(2,1)S(1)}, u32[]{:S(2)}, u32[]{:S(2)}) collective-permute-start(bf16[2,128,128]{2,1,0:T(8,128)(2,1)S(1)} %fusion.140), channel_id=1, source_target_pairs={{0,1},{1,2},{2,3},{3,4},{4,5},{5,6},{6,7},{7,8},{8,9},{9,10},{10,1... | collective-permute-start | bytes 196616 | tf_op jit(solution)/shard_map/while/body/eval_jaxpr/ppermute | solution.py:18
  186.2 5.6 %collective-permute-start = (bf16[2,128,128]{2,1,0:T(8,128)(2,1)S(1)}, bf16[2,128,128]{2,1,0:T(8,128)(2,1)S(1)}, u32[]{:S(2)}, u32[]{:S(2)}) collective-permute-start(bf16[2,128,128]{2,1,0:T(8,128)(2,1)S(1)} %fusion.140), channel_id=1, source_target_pairs={{0,1},{1,2},{2,3},{3,4},{4,5},{5,6},{6,7},{7,8},{8,9},{9,10},{10,1... | collective-permute-start | bytes 196616 | tf_op jit(solution)/shard_map/while/body/eval_jaxpr/ppermute | solution.py:18
  193.0 5.6 %collective-permute-start = (bf16[2,128,128]{2,1,0:T(8,128)(2,1)S(1)}, bf16[2,128,128]{2,1,0:T(8,128)(2,1)S(1)}, u32[]{:S(2)}, u32[]{:S(2)}) collective-permute-start(bf16[2,128,128]{2,1,0:T(8,128)(2,1)S(1)} %fusion.140), channel_id=1, source_target_pairs={{0,1},{1,2},{2,3},{3,4},{4,5},{5,6},{6,7},{7,8},{8,9},{9,10},{10,1... | collective-permute-start | bytes 196616 | tf_op jit(solution)/shard_map/while/body/eval_jaxpr/ppermute | solution.py:18
  199.8 5.6 %collective-permute-start = (bf16[2,128,128]{2,1,0:T(8,128)(2,1)S(1)}, bf16[2,128,128]{2,1,0:T(8,128)(2,1)S(1)}, u32[]{:S(2)}, u32[]{:S(2)}) collective-permute-start(bf16[2,128,128]{2,1,0:T(8,128)(2,1)S(1)} %fusion.140), channel_id=1, source_target_pairs={{0,1},{1,2},{2,3},{3,4},{4,5},{5,6},{6,7},{7,8},{8,9},{9,10},{10,1... | collective-permute-start | bytes 196616 | tf_op jit(solution)/shard_map/while/body/eval_jaxpr/ppermute | solution.py:18
  206.6 5.6 %collective-permute-start = (bf16[2,128,128]{2,1,0:T(8,128)(2,1)S(1)}, bf16[2,128,128]{2,1,0:T(8,128)(2,1)S(1)}, u32[]{:S(2)}, u32[]{:S(2)}) collective-permute-start(bf16[2,128,128]{2,1,0:T(8,128)(2,1)S(1)} %fusion.140), channel_id=1, source_target_pairs={{0,1},{1,2},{2,3},{3,4},{4,5},{5,6},{6,7},{7,8},{8,9},{9,10},{10,1... | collective-permute-start | bytes 196616 | tf_op jit(solution)/shard_map/while/body/eval_jaxpr/ppermute | solution.py:18
  213.4 5.6 %collective-permute-start = (bf16[2,128,128]{2,1,0:T(8,128)(2,1)S(1)}, bf16[2,128,128]{2,1,0:T(8,128)(2,1)S(1)}, u32[]{:S(2)}, u32[]{:S(2)}) collective-permute-start(bf16[2,128,128]{2,1,0:T(8,128)(2,1)S(1)} %fusion.140), channel_id=1, source_target_pairs={{0,1},{1,2},{2,3},{3,4},{4,5},{5,6},{6,7},{7,8},{8,9},{9,10},{10,1... | collective-permute-start | bytes 196616 | tf_op jit(solution)/shard_map/while/body/eval_jaxpr/ppermute | solution.py:18
  220.2 5.6 %collective-permute-start = (bf16[2,128,128]{2,1,0:T(8,128)(2,1)S(1)}, bf16[2,128,128]{2,1,0:T(8,128)(2,1)S(1)}, u32[]{:S(2)}, u32[]{:S(2)}) collective-permute-start(bf16[2,128,128]{2,1,0:T(8,128)(2,1)S(1)} %fusion.140), channel_id=1, source_target_pairs={{0,1},{1,2},{2,3},{3,4},{4,5},{5,6},{6,7},{7,8},{8,9},{9,10},{10,1... | collective-permute-start | bytes 196616 | tf_op jit(solution)/shard_map/while/body/eval_jaxpr/ppermute | solution.py:18
  227.0 5.6 %collective-permute-start = (bf16[2,128,128]{2,1,0:T(8,128)(2,1)S(1)}, bf16[2,128,128]{2,1,0:T(8,128)(2,1)S(1)}, u32[]{:S(2)}, u32[]{:S(2)}) collective-permute-start(bf16[2,128,128]{2,1,0:T(8,128)(2,1)S(1)} %fusion.140), channel_id=1, source_target_pairs={{0,1},{1,2},{2,3},{3,4},{4,5},{5,6},{6,7},{7,8},{8,9},{9,10},{10,1... | collective-permute-start | bytes 196616 | tf_op jit(solution)/shard_map/while/body/eval_jaxpr/ppermute | solution.py:18
  233.8 5.6 %collective-permute-start = (bf16[2,128,128]{2,1,0:T(8,128)(2,1)S(1)}, bf16[2,128,128]{2,1,0:T(8,128)(2,1)S(1)}, u32[]{:S(2)}, u32[]{:S(2)}) collective-permute-start(bf16[2,128,128]{2,1,0:T(8,128)(2,1)S(1)} %fusion.140), channel_id=1, source_target_pairs={{0,1},{1,2},{2,3},{3,4},{4,5},{5,6},{6,7},{7,8},{8,9},{9,10},{10,1... | collective-permute-start | bytes 196616 | tf_op jit(solution)/shard_map/while/body/eval_jaxpr/ppermute | solution.py:18
  240.6 5.6 %collective-permute-start = (bf16[2,128,128]{2,1,0:T(8,128)(2,1)S(1)}, bf16[2,128,128]{2,1,0:T(8,128)(2,1)S(1)}, u32[]{:S(2)}, u32[]{:S(2)}) collective-permute-start(bf16[2,128,128]{2,1,0:T(8,128)(2,1)S(1)} %fusion.140), channel_id=1, source_target_pairs={{0,1},{1,2},{2,3},{3,4},{4,5},{5,6},{6,7},{7,8},{8,9},{9,10},{10,1... | collective-permute-start | bytes 196616 | tf_op jit(solution)/shard_map/while/body/eval_jaxpr/ppermute | solution.py:18
  247.4 5.6 %collective-permute-start = (bf16[2,128,128]{2,1,0:T(8,128)(2,1)S(1)}, bf16[2,128,128]{2,1,0:T(8,128)(2,1)S(1)}, u32[]{:S(2)}, u32[]{:S(2)}) collective-permute-start(bf16[2,128,128]{2,1,0:T(8,128)(2,1)S(1)} %fusion.140), channel_id=1, source_target_pairs={{0,1},{1,2},{2,3},{3,4},{4,5},{5,6},{6,7},{7,8},{8,9},{9,10},{10,1... | collective-permute-start | bytes 196616 | tf_op jit(solution)/shard_map/while/body/eval_jaxpr/ppermute | solution.py:18
  254.2 6.1 %collective-permute-start = (bf16[2,128,128]{2,1,0:T(8,128)(2,1)S(1)}, bf16[2,128,128]{2,1,0:T(8,128)(2,1)S(1)}, u32[]{:S(2)}, u32[]{:S(2)}) collective-permute-start(bf16[2,128,128]{2,1,0:T(8,128)(2,1)S(1)} %fusion.140), channel_id=1, source_target_pairs={{0,1},{1,2},{2,3},{3,4},{4,5},{5,6},{6,7},{7,8},{8,9},{9,10},{10,1... | collective-permute-start | bytes 196616 | tf_op jit(solution)/shard_map/while/body/eval_jaxpr/ppermute | solution.py:18
  261.5 6.8 %collective-permute-start = (bf16[2,128,128]{2,1,0:T(8,128)(2,1)S(1)}, bf16[2,128,128]{2,1,0:T(8,128)(2,1)S(1)}, u32[]{:S(2)}, u32[]{:S(2)}) collective-permute-start(bf16[2,128,128]{2,1,0:T(8,128)(2,1)S(1)} %fusion.140), channel_id=1, source_target_pairs={{0,1},{1,2},{2,3},{3,4},{4,5},{5,6},{6,7},{7,8},{8,9},{9,10},{10,1... | collective-permute-start | bytes 196616 | tf_op jit(solution)/shard_map/while/body/eval_jaxpr/ppermute | solution.py:18
  269.5 6.8 %collective-permute-start = (bf16[2,128,128]{2,1,0:T(8,128)(2,1)S(1)}, bf16[2,128,128]{2,1,0:T(8,128)(2,1)S(1)}, u32[]{:S(2)}, u32[]{:S(2)}) collective-permute-start(bf16[2,128,128]{2,1,0:T(8,128)(2,1)S(1)} %fusion.140), channel_id=1, source_target_pairs={{0,1},{1,2},{2,3},{3,4},{4,5},{5,6},{6,7},{7,8},{8,9},{9,10},{10,1... | collective-permute-start | bytes 196616 | tf_op jit(solution)/shard_map/while/body/eval_jaxpr/ppermute | solution.py:18
  277.5 6.8 %collective-permute-start = (bf16[2,128,128]{2,1,0:T(8,128)(2,1)S(1)}, bf16[2,128,128]{2,1,0:T(8,128)(2,1)S(1)}, u32[]{:S(2)}, u32[]{:S(2)}) collective-permute-start(bf16[2,128,128]{2,1,0:T(8,128)(2,1)S(1)} %fusion.140), channel_id=1, source_target_pairs={{0,1},{1,2},{2,3},{3,4},{4,5},{5,6},{6,7},{7,8},{8,9},{9,10},{10,1... | collective-permute-start | bytes 196616 | tf_op jit(solution)/shard_map/while/body/eval_jaxpr/ppermute | solution.py:18
  285.5 6.8 %collective-permute-start = (bf16[2,128,128]{2,1,0:T(8,128)(2,1)S(1)}, bf16[2,128,128]{2,1,0:T(8,128)(2,1)S(1)}, u32[]{:S(2)}, u32[]{:S(2)}) collective-permute-start(bf16[2,128,128]{2,1,0:T(8,128)(2,1)S(1)} %fusion.140), channel_id=1, source_target_pairs={{0,1},{1,2},{2,3},{3,4},{4,5},{5,6},{6,7},{7,8},{8,9},{9,10},{10,1... | collective-permute-start | bytes 196616 | tf_op jit(solution)/shard_map/while/body/eval_jaxpr/ppermute | solution.py:18
  293.5 6.8 %collective-permute-start = (bf16[2,128,128]{2,1,0:T(8,128)(2,1)S(1)}, bf16[2,128,128]{2,1,0:T(8,128)(2,1)S(1)}, u32[]{:S(2)}, u32[]{:S(2)}) collective-permute-start(bf16[2,128,128]{2,1,0:T(8,128)(2,1)S(1)} %fusion.140), channel_id=1, source_target_pairs={{0,1},{1,2},{2,3},{3,4},{4,5},{5,6},{6,7},{7,8},{8,9},{9,10},{10,1... | collective-permute-start | bytes 196616 | tf_op jit(solution)/shard_map/while/body/eval_jaxpr/ppermute | solution.py:18
  301.5 6.8 %collective-permute-start = (bf16[2,128,128]{2,1,0:T(8,128)(2,1)S(1)}, bf16[2,128,128]{2,1,0:T(8,128)(2,1)S(1)}, u32[]{:S(2)}, u32[]{:S(2)}) collective-permute-start(bf16[2,128,128]{2,1,0:T(8,128)(2,1)S(1)} %fusion.140), channel_id=1, source_target_pairs={{0,1},{1,2},{2,3},{3,4},{4,5},{5,6},{6,7},{7,8},{8,9},{9,10},{10,1... | collective-permute-start | bytes 196616 | tf_op jit(solution)/shard_map/while/body/eval_jaxpr/ppermute | solution.py:18
  309.5 6.8 %collective-permute-start = (bf16[2,128,128]{2,1,0:T(8,128)(2,1)S(1)}, bf16[2,128,128]{2,1,0:T(8,128)(2,1)S(1)}, u32[]{:S(2)}, u32[]{:S(2)}) collective-permute-start(bf16[2,128,128]{2,1,0:T(8,128)(2,1)S(1)} %fusion.140), channel_id=1, source_target_pairs={{0,1},{1,2},{2,3},{3,4},{4,5},{5,6},{6,7},{7,8},{8,9},{9,10},{10,1... | collective-permute-start | bytes 196616 | tf_op jit(solution)/shard_map/while/body/eval_jaxpr/ppermute | solution.py:18
  317.5 6.8 %collective-permute-start = (bf16[2,128,128]{2,1,0:T(8,128)(2,1)S(1)}, bf16[2,128,128]{2,1,0:T(8,128)(2,1)S(1)}, u32[]{:S(2)}, u32[]{:S(2)}) collective-permute-start(bf16[2,128,128]{2,1,0:T(8,128)(2,1)S(1)} %fusion.140), channel_id=1, source_target_pairs={{0,1},{1,2},{2,3},{3,4},{4,5},{5,6},{6,7},{7,8},{8,9},{9,10},{10,1... | collective-permute-start | bytes 196616 | tf_op jit(solution)/shard_map/while/body/eval_jaxpr/ppermute | solution.py:18
  325.5 6.8 %collective-permute-start = (bf16[2,128,128]{2,1,0:T(8,128)(2,1)S(1)}, bf16[2,128,128]{2,1,0:T(8,128)(2,1)S(1)}, u32[]{:S(2)}, u32[]{:S(2)}) collective-permute-start(bf16[2,128,128]{2,1,0:T(8,128)(2,1)S(1)} %fusion.140), channel_id=1, source_target_pairs={{0,1},{1,2},{2,3},{3,4},{4,5},{5,6},{6,7},{7,8},{8,9},{9,10},{10,1... | collective-permute-start | bytes 196616 | tf_op jit(solution)/shard_map/while/body/eval_jaxpr/ppermute | solution.py:18
  333.5 6.8 %collective-permute-start = (bf16[2,128,128]{2,1,0:T(8,128)(2,1)S(1)}, bf16[2,128,128]{2,1,0:T(8,128)(2,1)S(1)}, u32[]{:S(2)}, u32[]{:S(2)}) collective-permute-start(bf16[2,128,128]{2,1,0:T(8,128)(2,1)S(1)} %fusion.140), channel_id=1, source_target_pairs={{0,1},{1,2},{2,3},{3,4},{4,5},{5,6},{6,7},{7,8},{8,9},{9,10},{10,1... | collective-permute-start | bytes 196616 | tf_op jit(solution)/shard_map/while/body/eval_jaxpr/ppermute | solution.py:18
  341.6 6.8 %collective-permute-start = (bf16[2,128,128]{2,1,0:T(8,128)(2,1)S(1)}, bf16[2,128,128]{2,1,0:T(8,128)(2,1)S(1)}, u32[]{:S(2)}, u32[]{:S(2)}) collective-permute-start(bf16[2,128,128]{2,1,0:T(8,128)(2,1)S(1)} %fusion.140), channel_id=1, source_target_pairs={{0,1},{1,2},{2,3},{3,4},{4,5},{5,6},{6,7},{7,8},{8,9},{9,10},{10,1... | collective-permute-start | bytes 196616 | tf_op jit(solution)/shard_map/while/body/eval_jaxpr/ppermute | solution.py:18
  349.6 6.8 %collective-permute-start = (bf16[2,128,128]{2,1,0:T(8,128)(2,1)S(1)}, bf16[2,128,128]{2,1,0:T(8,128)(2,1)S(1)}, u32[]{:S(2)}, u32[]{:S(2)}) collective-permute-start(bf16[2,128,128]{2,1,0:T(8,128)(2,1)S(1)} %fusion.140), channel_id=1, source_target_pairs={{0,1},{1,2},{2,3},{3,4},{4,5},{5,6},{6,7},{7,8},{8,9},{9,10},{10,1... | collective-permute-start | bytes 196616 | tf_op jit(solution)/shard_map/while/body/eval_jaxpr/ppermute | solution.py:18
  357.6 6.8 %collective-permute-start = (bf16[2,128,128]{2,1,0:T(8,128)(2,1)S(1)}, bf16[2,128,128]{2,1,0:T(8,128)(2,1)S(1)}, u32[]{:S(2)}, u32[]{:S(2)}) collective-permute-start(bf16[2,128,128]{2,1,0:T(8,128)(2,1)S(1)} %fusion.140), channel_id=1, source_target_pairs={{0,1},{1,2},{2,3},{3,4},{4,5},{5,6},{6,7},{7,8},{8,9},{9,10},{10,1... | collective-permute-start | bytes 196616 | tf_op jit(solution)/shard_map/while/body/eval_jaxpr/ppermute | solution.py:18
  365.6 6.8 %collective-permute-start = (bf16[2,128,128]{2,1,0:T(8,128)(2,1)S(1)}, bf16[2,128,128]{2,1,0:T(8,128)(2,1)S(1)}, u32[]{:S(2)}, u32[]{:S(2)}) collective-permute-start(bf16[2,128,128]{2,1,0:T(8,128)(2,1)S(1)} %fusion.140), channel_id=1, source_target_pairs={{0,1},{1,2},{2,3},{3,4},{4,5},{5,6},{6,7},{7,8},{8,9},{9,10},{10,1... | collective-permute-start | bytes 196616 | tf_op jit(solution)/shard_map/while/body/eval_jaxpr/ppermute | solution.py:18
  373.6 6.8 %collective-permute-start = (bf16[2,128,128]{2,1,0:T(8,128)(2,1)S(1)}, bf16[2,128,128]{2,1,0:T(8,128)(2,1)S(1)}, u32[]{:S(2)}, u32[]{:S(2)}) collective-permute-start(bf16[2,128,128]{2,1,0:T(8,128)(2,1)S(1)} %fusion.140), channel_id=1, source_target_pairs={{0,1},{1,2},{2,3},{3,4},{4,5},{5,6},{6,7},{7,8},{8,9},{9,10},{10,1... | collective-permute-start | bytes 196616 | tf_op jit(solution)/shard_map/while/body/eval_jaxpr/ppermute | solution.py:18
  (18 other events, 316.9 us)
Sparse Core Ops, SparseCore 0:
  10.3 62.7 all-gather.1
  413.0 110.0 reduce-scatter.3
where the time goes:
time: 535 us; the launch traced here: 531 us
  waiting for transfers between devices  194 us (36%)
  starting transfers between devices  163 us (30%)
  matrix products  83.5 us (16%)
  other arithmetic  55.4 us (10%)
  local copies, waits for them, and re-layouts  20.3 us (4%)
  between operations  13.7 us (3%)
    ppermute x32, starting transfers between devices, from_behind(): return lax.ppermute(array, axis, pairs)  163 us
    unnamed x3, waiting for transfers between devices  111 us
    all_gather x1, waiting for transfers between devices, local(): shard_piece = lax.all_gather(hidden, 'tensor', axis=1, tiled=True)  56.1 us
    another operation x4, other arithmetic, local(): jax.scipy.linalg.solve_triangular(system, (beta_blk * gammas)[..., None]...  42 us
    dot_general x31, matrix products, relay_step(): jnp.einsum('hvk,hkc->hvc', state_mat, dev_map, precision=PRECISE) + dev_add  36.5 us
    ppermute x32, waiting for transfers between devices, from_behind(): return lax.ppermute(array, axis, pairs)  27.3 us
  transfers between devices with their start and end apart: 34, of which 33 were waited for; matrix products, arithmetic and copies ran while one was open for 3% of the time, Pallas kernels for 0%

commit v1 on v0

v1 whole, which is shorter than its diff:
```python
import functools
import math

import jax
import jax.numpy as jnp
from jax import lax
from jax.experimental import pallas as pl
from jax.experimental.pallas import tpu as pltpu
from jax.sharding import PartitionSpec as P

F32 = jnp.float32
BF16 = jnp.bfloat16
TAIL = 16
VMEM_LIMIT = 48 * 1024 * 1024


def mm(a, b):
    return jnp.dot(a.astype(BF16), b.astype(BF16), preferred_element_type=F32)


def mm_nt(a, b):
    return lax.dot_general(
        a.astype(BF16), b.astype(BF16), (((1,), (1,)), ((), ())), preferred_element_type=F32
    )


def halves(a):
    high = a.astype(BF16)
    return high, (a - high.astype(F32)).astype(BF16)


def mm3(a, b):
    a_high, a_low = halves(a)
    b_high, b_low = halves(b)
    return (
        jnp.dot(a_high, b_high, preferred_element_type=F32)
        + jnp.dot(a_high, b_low, preferred_element_type=F32)
        + jnp.dot(a_low, b_high, preferred_element_type=F32)
    )


def silu(v):
    return v / (1.0 + jnp.exp(-v))


def project_kernel(x_ref, w_ref, wr_ref, mixed_ref, rates_ref, wide):
    parts, _, width = x_ref.shape
    for part in range(parts):
        wide[:, part * width : (part + 1) * width] = x_ref[part]
    x = wide[...]
    mixed_ref[...] = jnp.dot(x, w_ref[...], preferred_element_type=F32).astype(BF16)
    rates_ref[...] = jnp.dot(x, wr_ref[...], preferred_element_type=F32).astype(BF16)


def unit_lower_inverses(lowers, rows_at, cols_at):
    rows = lowers[0].shape[0]
    eye = (rows_at == cols_at).astype(F32)

    def between(lower, size):
        joins = ((rows_at // (2 * size)) == (cols_at // (2 * size))) & (
            (rows_at // size) != (cols_at // size)
        )
        return jnp.where(joins, lower, 0.0)

    found = [eye - between(lower, 1) for lower in lowers]
    size = 2
    while size < rows:
        halfway = [mm3(between(lower, size), t) for lower, t in zip(lowers, found)]
        found = [t - mm3(t, h) for t, h in zip(found, halfway)]
        size *= 2
    return found


def chunk_kernel(
    lens_ref,
    first_ref,
    rate_ref,
    bias_ref,
    mixed_ref,
    rim_ref,
    rates_ref,
    cw_ref,
    c_ref,
    m_ref,
    o_ref,
    ext,
):
    rows = mixed_ref.shape[0]
    dk = cw_ref.shape[1] // 4
    first = first_ref[0]
    pos = first + lax.broadcasted_iota(jnp.int32, (rows, 1), 0)
    start = jnp.zeros((rows, 1), jnp.int32)
    bound = jnp.int32(0)
    for i in range(lens_ref.shape[0] - 1):
        bound = bound + lens_ref[i]
        start = jnp.where(pos >= bound, bound, start)

    ext[0:TAIL, :] = rim_ref[...].astype(F32)
    ext[TAIL : TAIL + rows, :] = mixed_ref[:, : 4 * dk].astype(F32)
    conv = cw_ref[0:1, :] * ext[TAIL : TAIL + rows, :]
    for j in range(1, 4):
        keep = (pos - j >= start).astype(F32)
        conv = conv + cw_ref[j : j + 1, :] * (ext[TAIL - j : TAIL - j + rows, :] * keep)
    conv = silu(conv)
    q = conv[:, :dk]
    k = conv[:, dk : 2 * dk]
    q = q * (lax.rsqrt(jnp.sum(q * q, -1, keepdims=True) + 1e-6) * (1.0 / math.sqrt(dk)))
    k = k * lax.rsqrt(jnp.sum(k * k, -1, keepdims=True) + 1e-6)
    qb = q.astype(BF16)
    kb = k.astype(BF16)

    rates = rates_ref[...].astype(F32)
    betas = 1.0 / (1.0 + jnp.exp(-rates[:, 0:2]))
    lane2 = lax.broadcasted_iota(jnp.int32, (1, 2), 1)
    bias = jnp.where(lane2 == 0, bias_ref[0], bias_ref[1])
    decay = jnp.where(lane2 == 0, rate_ref[0], rate_ref[1])
    a_in = rates[:, 2:4] + bias
    steps = -decay * (jnp.maximum(a_in, 0.0) + jnp.log1p(jnp.exp(-jnp.abs(a_in))))

    rows_at = lax.broadcasted_iota(jnp.int32, (rows, rows), 0)
    cols_at = lax.broadcasted_iota(jnp.int32, (rows, rows), 1)
    lower = rows_at >= cols_at
    tri = lower.astype(BF16)
    lanes = lax.broadcasted_iota(jnp.int32, (1, dk), 1)
    padded = jnp.where(lanes == 0, steps[:, 0:1], jnp.where(lanes == 1, steps[:, 1:2], 0.0))
    p1 = padded.astype(BF16)
    r1 = padded - p1.astype(F32)
    p2 = r1.astype(BF16)
    p3 = (r1 - p2.astype(F32)).astype(BF16)
    cumul = (
        jnp.dot(tri, p1, preferred_element_type=F32)
        + jnp.dot(tri, p2, preferred_element_type=F32)
        + jnp.dot(tri, p3, preferred_element_type=F32)
    )
    cumul_t = jnp.transpose(cumul)

    visible = lower & (cols_at + first >= start)
    gram = mm_nt(kb, kb)
    cross = mm_nt(qb, kb)
    last_start = start[rows - 1 : rows, :]
    carries = (start < first).astype(F32)
    in_tail = (pos >= last_start).astype(F32)

    lowers, scores = [], []
    for h in range(2):
        differ = cumul[:, h : h + 1] - cumul_t[h : h + 1, :]
        ratio = jnp.where(visible, jnp.exp(jnp.where(visible, differ, 0.0)), 0.0)
        scores.append(cross * ratio)
        lowers.append(
            jnp.where(rows_at > cols_at, betas[:, h : h + 1] * ratio * gram, 0.0)
        )
    inverses = unit_lower_inverses(lowers, rows_at, cols_at)
    square = lax.broadcasted_iota(jnp.int32, (dk, 2 * dk), 0)
    across = lax.broadcasted_iota(jnp.int32, (dk, 2 * dk), 1)
    for h in range(2):
        col = cumul[:, h : h + 1]
        beta = betas[:, h : h + 1]
        gamma = jnp.exp(col) * carries
        value = conv[:, (2 + h) * dk : (3 + h) * dk]
        rhs = jnp.concatenate([(beta * gamma) * k, beta * value], axis=1)
        wu = mm(inverses[h], rhs)
        last = col[rows - 1 : rows, :]
        tail = jnp.exp(last - col) * in_tail
        k_tail = jnp.transpose(k * tail)
        made = mm(k_tail, wu)
        gamma_last = gamma[rows - 1 : rows, :]
        c_ref[h] = (
            jnp.where(square == across, gamma_last, 0.0) + jnp.where(across < dk, -made, made)
        ).astype(BF16)
        both = mm(scores[h], wu)
        m_ref[h] = (gamma * q - both[:, :dk]).astype(BF16)
        o_ref[h] = both[:, dk:]


def compose(late, early):
    dk = late.shape[0]
    made = jnp.dot(late[:, :dk], early, preferred_element_type=F32)
    across = lax.broadcasted_iota(jnp.int32, made.shape, 1)
    return made + jnp.where(across < dk, 0.0, late.astype(F32))


def compose_kernel(late_ref, early_ref, out_ref):
    for h in range(2):
        out_ref[h] = compose(late_ref[h], early_ref[h]).astype(BF16)


def finish_kernel(near_ref, far_ref, m_ref, o_ref, gate_ref, gain_ref, w_ref, out_ref):
    dk = gain_ref.shape[1]
    parts, _, width = out_ref.shape
    sides = []
    for h in range(2):
        near = near_ref[h]
        state = jnp.dot(near[:, :dk], far_ref[h], preferred_element_type=F32)
        state = state + near[:, dk:].astype(F32)
        rec = o_ref[h] + jnp.dot(m_ref[h], state.astype(BF16), preferred_element_type=F32)
        scale = lax.rsqrt(jnp.mean(rec * rec, -1, keepdims=True) + 1e-6)
        gate = silu(gate_ref[:, h * dk : (h + 1) * dk].astype(F32))
        sides.append((rec * scale * gain_ref[...] * gate).astype(BF16))
    normed = jnp.concatenate(sides, axis=1)
    share = jnp.dot(normed, w_ref[...], preferred_element_type=F32).astype(BF16)
    for part in range(parts):
        out_ref[part] = share[:, part * width : (part + 1) * width]


def vmem():
    return pl.BlockSpec(memory_space=pltpu.VMEM)


def smem():
    return pl.BlockSpec(memory_space=pltpu.SMEM)


def params():
    return pltpu.CompilerParams(vmem_limit_bytes=VMEM_LIMIT)


def shifted(array, by):
    peers = lax.axis_size("context")
    return lax.ppermute(array, "context", [(i, i + by) for i in range(peers - by)])


def local(
    hidden,
    proj_qkvz,
    proj_rates,
    conv_weight,
    decay_rate,
    step_bias,
    norm_gain,
    proj_out,
    doc_lengths,
):
    rows, width = hidden.shape
    dk = norm_gain.shape[0]
    peers = lax.axis_size("tensor")
    first = (lax.axis_index("context") * rows).astype(jnp.int32).reshape(1)
    shape = jax.ShapeDtypeStruct

    spread = jnp.broadcast_to(hidden[None], (peers, rows, width))
    gathered = lax.all_to_all(spread, "tensor", 0, 0, tiled=True)
    mixed, rates = pl.pallas_call(
        project_kernel,
        out_shape=(shape((rows, 6 * dk), BF16), shape((rows, 4), BF16)),
        in_specs=[vmem()] * 3,
        out_specs=(vmem(), vmem()),
        scratch_shapes=[pltpu.VMEM((rows, peers * width), BF16)],
        compiler_params=params(),
    )(gathered, proj_qkvz, proj_rates)
    rim = shifted(mixed[rows - TAIL :, : 4 * dk], 1)

    summary, follow, own = pl.pallas_call(
        chunk_kernel,
        out_shape=(
            shape((2, dk, 2 * dk), BF16),
            shape((2, rows, dk), BF16),
            shape((2, rows, dk), F32),
        ),
        in_specs=[smem()] * 4 + [vmem()] * 4,
        out_specs=(vmem(), vmem(), vmem()),
        scratch_shapes=[pltpu.VMEM((rows + TAIL, 4 * dk), F32)],
        compiler_params=params(),
    )(
        doc_lengths,
        first,
        decay_rate,
        step_bias,
        mixed,
        rim,
        rates,
        conv_weight.reshape(4, 4 * dk),
    )

    def joined(late, early):
        return pl.pallas_call(
            compose_kernel,
            out_shape=shape((2, dk, 2 * dk), BF16),
            in_specs=[vmem()] * 2,
            out_specs=vmem(),
            compiler_params=params(),
        )(late, early)

    window = joined(shifted(summary, 1), shifted(summary, 2))
    window = joined(window, shifted(window, 2))
    window = joined(window, shifted(window, 4))
    far = shifted(window[:, :, dk:], 8)

    share = pl.pallas_call(
        finish_kernel,
        out_shape=shape((peers, rows, width), BF16),
        in_specs=[vmem()] * 7,
        out_specs=vmem(),
        compiler_params=params(),
    )(window, far, follow, own, mixed[:, 4 * dk :], norm_gain.reshape(1, dk), proj_out)
    shares = lax.all_to_all(share, "tensor", 0, 0, tiled=True)
    return jnp.sum(shares.astype(F32), axis=0).astype(BF16)


def solution(mesh):
    placed = (
        P("context", "tensor"),
        P(None, "tensor"),
        P(None, "tensor"),
        P(None, "tensor", None),
        P("tensor"),
        P("tensor"),
        P(),
        P("tensor", None),
        P(),
    )
    return jax.shard_map(
        local, mesh=mesh, in_specs=placed, out_specs=P("context", "tensor"), check_vma=False
    )
```

time: 535 us -> 107 us (0.20)
  the two profiles are of different devices: /device:TPU:2 before, /device:TPU:96 now
where the time goes in v1:
time: 107 us; the launch traced here: 106 us
  starting transfers between devices  37.2 us (35%)
  waiting for transfers between devices  34.8 us (33%)
  blocking collectives  19.3 us (18%)
  Pallas kernels  9.62 us (9%)
  local copies, waits for them, and re-layouts  4.3 us (4%)
    ppermute x6, starting transfers between devices, shifted(): lax.ppermute(array, 'context', [(i, i + by) for i in range(peers - by)])  30.1 us
    all_to_all x1, blocking collectives, local(): shares = lax.all_to_all(share, 'tensor', 0, 0, tiled=True)  19.3 us
    ppermute x6, waiting for transfers between devices, shifted(): lax.ppermute(array, 'context', [(i, i + by) for i in range(peers - by)])  17.5 us
    all_to_all x1, waiting for transfers between devices, local(): gathered = lax.all_to_all(spread, 'tensor', 0, 0, tiled=True)  17.3 us
    pallas_call x1, Pallas kernels, local(): pl.pallas_call(chunk_kernel, out_shape=(shape((2, dk, 2 * dk), BF16), sha...  7.04 us
    all_to_all x1, starting transfers between devices, local(): gathered = lax.all_to_all(spread, 'tensor', 0, 0, tiled=True)  7.03 us
    unnamed x18, local copies, waits for them, and re-layouts  2.24 us
  transfers between devices with their start and end apart: 7, of which 6 were waited for; matrix products, arithmetic and copies ran while one was open for 0% of the time, Pallas kernels for 0%

profile of v1, /device:TPU:96, one launch (start us, length us, event | category | flops | bytes accessed | tf_op | source)
XLA Modules:
  0.0 106.1 jit_solution(17250606827760828132)
XLA Ops:
  0.0 2.0 %broadcast_in_dim.2 = bf16[16,256,128]{2,1,0:T(8,128)(2,1)} broadcast(bf16[256,128]{1,0:T(8,128)(2,1)} %param.9), dimensions={1,2} | broadcast | bytes 1114112 | tf_op jit(solution)/shard_map/broadcast_in_dim | solution.py:239
  2.0 7.0 %all-to-all-start = ((bf16[16,256,128]{2,1,0:T(8,128)(2,1)}), bf16[16,256,128]{2,1,0:T(8,128)(2,1)S(1)}, u32[]{:S(2)}, u32[]{:S(2)}) async-start(bf16[16,256,128]{2,1,0:T(8,128)(2,1)} %broadcast_in_dim.2), calls=%async_computation | async-start | bytes 2097152 | tf_op jit(solution)/shard_map/all_to_all | solution.py:240
  9.1 0.0 copy-done.6
  9.1 0.0 copy-start.7
  9.1 0.0 copy-start.3
  9.1 0.0 copy-start.4
  9.1 0.0 copy-start.5
  9.1 0.3 copy.10.wr_ref
  9.5 17.3 %all-to-all-done.x_ref = bf16[16,256,128]{2,1,0:T(8,128)(2,1)S(1)} async-done(((bf16[16,256,128]{2,1,0:T(8,128)(2,1)}), bf16[16,256,128]{2,1,0:T(8,128)(2,1)S(1)}, u32[]{:S(2)}, u32[]{:S(2)}) %all-to-all-start) | async-done | bytes 1048608 | tf_op jit(solution)/shard_map/all_to_all | solution.py:240
  26.7 1.9 %copy-done = bf16[2048,768]{1,0:T(8,128)(2,1)S(1)} copy-done((bf16[2048,768]{1,0:T(8,128)(2,1)S(1)}, bf16[2048,768]{1,0:T(8,128)(2,1)}, u32[]{:S(2)}) %copy-start) | copy-done | bytes 3145752
  28.6 1.3 %shard_map.91 = (bf16[256,768]{1,0:T(8,128)(2,1)S(1)}, bf16[256,4]{1,0:T(8,128)(2,1)S(1)}) custom-call(bf16[16,256,128]{2,1,0:T(8,128)(2,1)S(1)} %all-to-all-done.x_ref, bf16[2048,768]{1,0:T(8,128)(2,1)S(1)} %copy-done, bf16[2048,4]{1,0:T(8,128)(2,1)S(1)} %copy.10.wr_ref), custom_call_target="tpu_custom_call" | custom-call | tf_op jit(solution)/shard_map/pallas_call | solution.py:241
  29.9 1.9 %collective-permute-start = (bf16[16,512]{1,0:T(8,128)(2,1)S(1)}, bf16[16,512]{1,0:T(8,128)(2,1)S(1)}, u32[]{:S(2)}, u32[]{:S(2)}) collective-permute-start(bf16[16,512]{1,0:T(8,128)(2,1)S(1)} %slice.9), channel_id=1, source_target_pairs={{0,1},{1,2},{2,3},{3,4},{4,5},{5,6},{6,7},{7,8},{8,9},{9,10},{10,1... | collective-permute-start | bytes 49160 | tf_op jit(solution)/shard_map/ppermute | solution.py:219
  31.8 0.0 copy-done.7
  31.9 3.1 %collective-permute-done.rim_ref = bf16[16,512]{1,0:T(8,128)(2,1)S(1)} collective-permute-done((bf16[16,512]{1,0:T(8,128)(2,1)S(1)}, bf16[16,512]{1,0:T(8,128)(2,1)S(1)}, u32[]{:S(2)}, u32[]{:S(2)}) %collective-permute-start) | collective-permute-done | bytes 16416 | tf_op jit(solution)/shard_map/ppermute | solution.py:219
  35.0 0.0 copy-done.3
  35.0 7.0 %shard_map.92 = (bf16[2,128,256]{2,1,0:T(8,128)(2,1)S(1)}, bf16[2,256,128]{2,1,0:T(8,128)(2,1)S(1)}, f32[2,256,128]{2,1,0:T(8,128)S(1)}) custom-call(s32[8]{0:T(128)S(1)} %copy-done.3, s32[1]{0:T(128)} %bitcast.first_ref, f32[2]{0:T(128)S(1)} %copy-done.4, f32[2]{0:T(128)S(1)} %copy-done.5, bf16[256,768]{1,0:T(8,128)(2,1)S(1)} %get-tuple-element.10.mixed_ref, ...), custom_call_target="tpu_custom_call" | custom-call | tf_op jit(solution)/shard_map/pallas_call | solution.py:251
  42.0 2.9 %collective-permute-start.1 = (bf16[2,128,256]{2,1,0:T(8,128)(2,1)S(1)}, bf16[2,128,256]{2,1,0:T(8,128)(2,1)S(1)}, u32[]{:S(2)}, u32[]{:S(2)}) collective-permute-start(bf16[2,128,256]{2,1,0:T(8,128)(2,1)S(1)} %get-tuple-element.12), channel_id=1, source_target_pairs={{0,1},{1,2},{2,3},{3,4},{4,5},{5,6},{6,7},{7,8},{8,9},{9,10},{10,1... | collective-permute-start | bytes 393224 | tf_op jit(solution)/shard_map/ppermute | solution.py:219
  44.9 5.3 %collective-permute-start.2 = (bf16[2,128,256]{2,1,0:T(8,128)(2,1)S(1)}, bf16[2,128,256]{2,1,0:T(8,128)(2,1)S(1)}, u32[]{:S(2)}, u32[]{:S(2)}) collective-permute-start(bf16[2,128,256]{2,1,0:T(8,128)(2,1)S(1)} %get-tuple-element.12), channel_id=1, source_target_pairs={{0,2},{1,3},{2,4},{3,5},{4,6},{5,7},{6,8},{7,9},{8,10},{9,11},{10,... | collective-permute-start | bytes 393224 | tf_op jit(solution)/shard_map/ppermute | solution.py:219
  50.2 0.0 collective-permute-done.1.late_ref
  50.2 3.7 %collective-permute-done.2.early_ref = bf16[2,128,256]{2,1,0:T(8,128)(2,1)S(1)} collective-permute-done((bf16[2,128,256]{2,1,0:T(8,128)(2,1)S(1)}, bf16[2,128,256]{2,1,0:T(8,128)(2,1)S(1)}, u32[]{:S(2)}, u32[]{:S(2)}) %collective-permute-start.2) | collective-permute-done | bytes 131104 | tf_op jit(solution)/shard_map/ppermute | solution.py:219
  53.9 0.2 shard_map.93.late_ref
  54.1 5.6 %collective-permute-start.3 = (bf16[2,128,256]{2,1,0:T(8,128)(2,1)S(1)}, bf16[2,128,256]{2,1,0:T(8,128)(2,1)S(1)}, u32[]{:S(2)}, u32[]{:S(2)}) collective-permute-start(bf16[2,128,256]{2,1,0:T(8,128)(2,1)S(1)} %shard_map.93.late_ref), channel_id=1, source_target_pairs={{0,2},{1,3},{2,4},{3,5},{4,6},{5,7},{6,8},{7,9},{8,10},{9,11},{10,... | collective-permute-start | bytes 393224 | tf_op jit(solution)/shard_map/ppermute | solution.py:219
  59.7 2.9 %collective-permute-done.3.early_ref = bf16[2,128,256]{2,1,0:T(8,128)(2,1)S(1)} collective-permute-done((bf16[2,128,256]{2,1,0:T(8,128)(2,1)S(1)}, bf16[2,128,256]{2,1,0:T(8,128)(2,1)S(1)}, u32[]{:S(2)}, u32[]{:S(2)}) %collective-permute-start.3) | collective-permute-done | bytes 131104 | tf_op jit(solution)/shard_map/ppermute | solution.py:219
  62.6 0.2 shard_map.94.late_ref
  62.8 4.1 %collective-permute-start.4 = (bf16[2,128,256]{2,1,0:T(8,128)(2,1)S(1)}, bf16[2,128,256]{2,1,0:T(8,128)(2,1)S(1)}, u32[]{:S(2)}, u32[]{:S(2)}) collective-permute-start(bf16[2,128,256]{2,1,0:T(8,128)(2,1)S(1)} %shard_map.94.late_ref), channel_id=1, source_target_pairs={{0,4},{1,5},{2,6},{3,7},{4,8},{5,9},{6,10},{7,11},{8,12},{9,13},{1... | collective-permute-start | bytes 393224 | tf_op jit(solution)/shard_map/ppermute | solution.py:219
  66.9 4.5 %collective-permute-done.4.early_ref = bf16[2,128,256]{2,1,0:T(8,128)(2,1)S(1)} collective-permute-done((bf16[2,128,256]{2,1,0:T(8,128)(2,1)S(1)}, bf16[2,128,256]{2,1,0:T(8,128)(2,1)S(1)}, u32[]{:S(2)}, u32[]{:S(2)}) %collective-permute-start.4) | collective-permute-done | bytes 131104 | tf_op jit(solution)/shard_map/ppermute | solution.py:219
  71.4 0.2 shard_map.95.near_ref
  71.6 10.3 %collective-permute-start.5 = (bf16[2,128,128]{2,1,0:T(8,128)(2,1)S(1)}, bf16[2,128,128]{2,1,0:T(8,128)(2,1)S(1)}, u32[]{:S(2)}, u32[]{:S(2)}) collective-permute-start(bf16[2,128,128]{2,1,0:T(8,128)(2,1)S(1)} %slice.12), channel_id=1, source_target_pairs={{0,8},{1,9},{2,10},{3,11},{4,12},{5,13},{6,14},{7,15},{8,16},{9,17... | collective-permute-start | bytes 196616 | tf_op jit(solution)/shard_map/ppermute | solution.py:219
  81.9 3.3 %collective-permute-done.5.far_ref = bf16[2,128,128]{2,1,0:T(8,128)(2,1)S(1)} collective-permute-done((bf16[2,128,128]{2,1,0:T(8,128)(2,1)S(1)}, bf16[2,128,128]{2,1,0:T(8,128)(2,1)S(1)}, u32[]{:S(2)}, u32[]{:S(2)}) %collective-permute-start.5) | collective-permute-done | bytes 65568 | tf_op jit(solution)/shard_map/ppermute | solution.py:219
  85.2 0.8 shard_map.96
  86.1 19.3 %all_to_all.10 = bf16[16,256,128]{2,1,0:T(8,128)(2,1)S(1)} all-to-all(bf16[16,256,128]{2,1,0:T(8,128)(2,1)S(1)} %shard_map.96), channel_id=1, replica_groups=mesh['tensor'=16,'context'=32] {'tensor'}, dimensions={0} | all-to-all | bytes 2097152 | tf_op jit(solution)/shard_map/all_to_all | solution.py:294
  105.3 0.8 reduce_sum.12
  (12 shorter events, 0.0 us)
Async XLA Ops:
  0.0 9.1 %copy-start.6 = (bf16[2048,4]{0,1:T(4,128)(2,1)S(1)}, bf16[2048,4]{0,1:T(4,128)(2,1)}, u32[]{:S(2)}) copy-start(bf16[2048,4]{0,1:T(4,128)(2,1)} %param.11) | copy-start | bytes 49156
  2.0 24.7 %all-to-all-start = ((bf16[16,256,128]{2,1,0:T(8,128)(2,1)}), bf16[16,256,128]{2,1,0:T(8,128)(2,1)S(1)}, u32[]{:S(2)}, u32[]{:S(2)}) async-start(bf16[16,256,128]{2,1,0:T(8,128)(2,1)} %broadcast_in_dim.2), calls=%async_computation | async-start | bytes 2097152 | tf_op jit(solution)/shard_map/all_to_all | solution.py:240
  9.1 22.7 %copy-start.7 = (f32[4,1,512]{2,1,0:T(1,128)S(1)}, f32[4,1,512]{2,1,0:T(1,128)}, u32[]{:S(2)}) copy-start(f32[4,1,512]{2,1,0:T(1,128)} %param.12) | copy-start | bytes 24580
  9.1 25.9 %copy-start.3 = (s32[8]{0:T(128)S(1)}, s32[8]{0:T(128)}, u32[]{:S(2)}) copy-start(s32[8]{0:T(128)} %lens_ref.1) | copy-start | bytes 100
  9.1 25.8 %copy-start.4 = (f32[2]{0:T(128)S(1)}, f32[2]{0:T(128)}, u32[]{:S(2)}) copy-start(f32[2]{0:T(128)} %rate_ref.1) | copy-start | bytes 28
  9.1 25.8 %copy-start.5 = (f32[2]{0:T(128)S(1)}, f32[2]{0:T(128)}, u32[]{:S(2)}) copy-start(f32[2]{0:T(128)} %bias_ref.1) | copy-start | bytes 28
  26.7 1.9 %copy-start = (bf16[2048,768]{1,0:T(8,128)(2,1)S(1)}, bf16[2048,768]{1,0:T(8,128)(2,1)}, u32[]{:S(2)}) copy-start(bf16[2048,768]{1,0:T(8,128)(2,1)} %w_ref.2) | copy-start | bytes 9437188
  28.6 56.6 %copy-start.1 = (bf16[256,2048]{1,0:T(8,128)(2,1)S(1)}, bf16[256,2048]{1,0:T(8,128)(2,1)}, u32[]{:S(2)}) copy-start(bf16[256,2048]{1,0:T(8,128)(2,1)} %w_ref.3) | copy-start | bytes 3145732
  28.6 56.6 %copy-start.2 = (f32[128]{0:T(128)S(1)}, f32[128]{0:T(128)}, u32[]{:S(2)}) copy-start(f32[128]{0:T(128)} %param.15) | copy-start | bytes 1540
  29.9 5.1 %collective-permute-start = (bf16[16,512]{1,0:T(8,128)(2,1)S(1)}, bf16[16,512]{1,0:T(8,128)(2,1)S(1)}, u32[]{:S(2)}, u32[]{:S(2)}) collective-permute-start(bf16[16,512]{1,0:T(8,128)(2,1)S(1)} %slice.9), channel_id=1, source_target_pairs={{0,1},{1,2},{2,3},{3,4},{4,5},{5,6},{6,7},{7,8},{8,9},{9,10},{10,1... | collective-permute-start | bytes 49160 | tf_op jit(solution)/shard_map/ppermute | solution.py:219
  42.0 8.2 %collective-permute-start.1 = (bf16[2,128,256]{2,1,0:T(8,128)(2,1)S(1)}, bf16[2,128,256]{2,1,0:T(8,128)(2,1)S(1)}, u32[]{:S(2)}, u32[]{:S(2)}) collective-permute-start(bf16[2,128,256]{2,1,0:T(8,128)(2,1)S(1)} %get-tuple-element.12), channel_id=1, source_target_pairs={{0,1},{1,2},{2,3},{3,4},{4,5},{5,6},{6,7},{7,8},{8,9},{9,10},{10,1... | collective-permute-start | bytes 393224 | tf_op jit(solution)/shard_map/ppermute | solution.py:219
  44.9 9.0 %collective-permute-start.2 = (bf16[2,128,256]{2,1,0:T(8,128)(2,1)S(1)}, bf16[2,128,256]{2,1,0:T(8,128)(2,1)S(1)}, u32[]{:S(2)}, u32[]{:S(2)}) collective-permute-start(bf16[2,128,256]{2,1,0:T(8,128)(2,1)S(1)} %get-tuple-element.12), channel_id=1, source_target_pairs={{0,2},{1,3},{2,4},{3,5},{4,6},{5,7},{6,8},{7,9},{8,10},{9,11},{10,... | collective-permute-start | bytes 393224 | tf_op jit(solution)/shard_map/ppermute | solution.py:219
  54.1 8.5 %collective-permute-start.3 = (bf16[2,128,256]{2,1,0:T(8,128)(2,1)S(1)}, bf16[2,128,256]{2,1,0:T(8,128)(2,1)S(1)}, u32[]{:S(2)}, u32[]{:S(2)}) collective-permute-start(bf16[2,128,256]{2,1,0:T(8,128)(2,1)S(1)} %shard_map.93.late_ref), channel_id=1, source_target_pairs={{0,2},{1,3},{2,4},{3,5},{4,6},{5,7},{6,8},{7,9},{8,10},{9,11},{10,... | collective-permute-start | bytes 393224 | tf_op jit(solution)/shard_map/ppermute | solution.py:219
  62.8 8.6 %collective-permute-start.4 = (bf16[2,128,256]{2,1,0:T(8,128)(2,1)S(1)}, bf16[2,128,256]{2,1,0:T(8,128)(2,1)S(1)}, u32[]{:S(2)}, u32[]{:S(2)}) collective-permute-start(bf16[2,128,256]{2,1,0:T(8,128)(2,1)S(1)} %shard_map.94.late_ref), channel_id=1, source_target_pairs={{0,4},{1,5},{2,6},{3,7},{4,8},{5,9},{6,10},{7,11},{8,12},{9,13},{1... | collective-permute-start | bytes 393224 | tf_op jit(solution)/shard_map/ppermute | solution.py:219
  71.6 13.6 %collective-permute-start.5 = (bf16[2,128,128]{2,1,0:T(8,128)(2,1)S(1)}, bf16[2,128,128]{2,1,0:T(8,128)(2,1)S(1)}, u32[]{:S(2)}, u32[]{:S(2)}) collective-permute-start(bf16[2,128,128]{2,1,0:T(8,128)(2,1)S(1)} %slice.12), channel_id=1, source_target_pairs={{0,8},{1,9},{2,10},{3,11},{4,12},{5,13},{6,14},{7,15},{8,16},{9,17... | collective-permute-start | bytes 196616 | tf_op jit(solution)/shard_map/ppermute | solution.py:219

commit v2 on v1

--- a/solution.py
+++ b/solution.py
@@ -24,32 +24,22 @@
     )
 
 
-def halves(a):
-    high = a.astype(BF16)
-    return high, (a - high.astype(F32)).astype(BF16)
-
-
-def mm3(a, b):
-    a_high, a_low = halves(a)
-    b_high, b_low = halves(b)
-    return (
-        jnp.dot(a_high, b_high, preferred_element_type=F32)
-        + jnp.dot(a_high, b_low, preferred_element_type=F32)
-        + jnp.dot(a_low, b_high, preferred_element_type=F32)
-    )
-
-
 def silu(v):
     return v / (1.0 + jnp.exp(-v))
 
 
-def project_kernel(x_ref, w_ref, wr_ref, mixed_ref, rates_ref, wide):
-    parts, _, width = x_ref.shape
-    for part in range(parts):
-        wide[:, part * width : (part + 1) * width] = x_ref[part]
-    x = wide[...]
-    mixed_ref[...] = jnp.dot(x, w_ref[...], preferred_element_type=F32).astype(BF16)
-    rates_ref[...] = jnp.dot(x, wr_ref[...], preferred_element_type=F32).astype(BF16)
+def spread_kernel(x_ref, rim_ref, out_ref):
+    block = x_ref[...]
+    rim = rim_ref[...]
+    for part in range(out_ref.shape[0]):
+        out_ref[part, 0:TAIL, :] = rim
+        out_ref[part, TAIL:, :] = block
+
+
+def stage_kernel(w_ref, out_ref, sem):
+    copy = pltpu.make_async_copy(w_ref, out_ref, sem)
+    copy.start()
+    copy.wait()
 
 
 def unit_lower_inverses(lowers, rows_at, cols_at):
@@ -65,8 +55,8 @@
     found = [eye - between(lower, 1) for lower in lowers]
     size = 2
     while size < rows:
-        halfway = [mm3(between(lower, size), t) for lower, t in zip(lowers, found)]
-        found = [t - mm3(t, h) for t, h in zip(found, halfway)]
+        halfway = [mm(between(lower, size), t) for lower, t in zip(lowers, found)]
+        found = [t - mm(t, h) for t, h in zip(found, halfway)]
         size *= 2
     return found
 
@@ -76,17 +66,26 @@
     first_ref,
     rate_ref,
     bias_ref,
-    mixed_ref,
-    rim_ref,
-    rates_ref,
+    x_ref,
+    w_ref,
+    wr_ref,
     cw_ref,
     c_ref,
     m_ref,
     o_ref,
+    z_ref,
+    wide,
     ext,
 ):
-    rows = mixed_ref.shape[0]
-    dk = cw_ref.shape[1] // 4
+    parts, rows, width = x_ref.shape
+    rows = rows - TAIL
+    dk = cw_ref.shape[2] // 4
+    for part in range(parts):
+        wide[:, part * width : (part + 1) * width] = x_ref[part]
+    mixed = jnp.dot(wide[...], w_ref[...], preferred_element_type=F32)
+    ext[...] = mixed[:, : 4 * dk].astype(BF16).astype(F32)
+    z_ref[...] = mixed[TAIL : TAIL + rows, 4 * dk :].astype(BF16)
+    rates = mm_nt(wide[TAIL : TAIL + rows, :], wr_ref[...]).astype(BF16).astype(F32)
     first = first_ref[0]
     pos = first + lax.broadcasted_iota(jnp.int32, (rows, 1), 0)
     start = jnp.zeros((rows, 1), jnp.int32)
@@ -95,12 +94,10 @@
         bound = bound + lens_ref[i]
         start = jnp.where(pos >= bound, bound, start)
 
-    ext[0:TAIL, :] = rim_ref[...].astype(F32)
-    ext[TAIL : TAIL + rows, :] = mixed_ref[:, : 4 * dk].astype(F32)
-    conv = cw_ref[0:1, :] * ext[TAIL : TAIL + rows, :]
+    conv = cw_ref[0] * ext[TAIL : TAIL + rows, :]
     for j in range(1, 4):
         keep = (pos - j >= start).astype(F32)
-        conv = conv + cw_ref[j : j + 1, :] * (ext[TAIL - j : TAIL - j + rows, :] * keep)
+        conv = conv + cw_ref[j] * (ext[TAIL - j : TAIL - j + rows, :] * keep)
     conv = silu(conv)
     q = conv[:, :dk]
     k = conv[:, dk : 2 * dk]
@@ -109,7 +106,6 @@
     qb = q.astype(BF16)
     kb = k.astype(BF16)
 
-    rates = rates_ref[...].astype(F32)
     betas = 1.0 / (1.0 + jnp.exp(-rates[:, 0:2]))
     lane2 = lax.broadcasted_iota(jnp.int32, (1, 2), 1)
     bias = jnp.where(lane2 == 0, bias_ref[0], bias_ref[1])
@@ -236,38 +232,49 @@
     first = (lax.axis_index("context") * rows).astype(jnp.int32).reshape(1)
     shape = jax.ShapeDtypeStruct
 
-    spread = jnp.broadcast_to(hidden[None], (peers, rows, width))
+    tail = shifted(hidden[rows - TAIL :], 1)
+    spread = pl.pallas_call(
+        spread_kernel,
+        out_shape=shape((peers, TAIL + rows, width), BF16),
+        in_specs=[vmem()] * 2,
+        out_specs=vmem(),
+        compiler_params=params(),
+    )(hidden, tail)
+    staged = pl.pallas_call(
+        stage_kernel,
+        out_shape=shape(proj_qkvz.shape, BF16),
+        in_specs=[pl.BlockSpec(memory_space=pl.ANY)],
+        out_specs=vmem(),
+        scratch_shapes=[pltpu.SemaphoreType.DMA],
+        compiler_params=params(),
+    )(proj_qkvz)
+    spread, staged, first = lax.optimization_barrier((spread, staged, first))
     gathered = lax.all_to_all(spread, "tensor", 0, 0, tiled=True)
-    mixed, rates = pl.pallas_call(
-        project_kernel,
-        out_shape=(shape((rows, 6 * dk), BF16), shape((rows, 4), BF16)),
-        in_specs=[vmem()] * 3,
-        out_specs=(vmem(), vmem()),
-        scratch_shapes=[pltpu.VMEM((rows, peers * width), BF16)],
-        compiler_params=params(),
-    )(gathered, proj_qkvz, proj_rates)
-    rim = shifted(mixed[rows - TAIL :, : 4 * dk], 1)
-
-    summary, follow, own = pl.pallas_call(
+
+    summary, follow, own, gate = pl.pallas_call(
         chunk_kernel,
         out_shape=(
             shape((2, dk, 2 * dk), BF16),
             shape((2, rows, dk), BF16),
             shape((2, rows, dk), F32),
+            shape((rows, 2 * dk), BF16),
         ),
         in_specs=[smem()] * 4 + [vmem()] * 4,
-        out_specs=(vmem(), vmem(), vmem()),
-        scratch_shapes=[pltpu.VMEM((rows + TAIL, 4 * dk), F32)],
+        out_specs=(vmem(),) * 4,
+        scratch_shapes=[
+            pltpu.VMEM((rows + TAIL, peers * width), BF16),
+            pltpu.VMEM((rows + TAIL, 4 * dk), F32),
+        ],
         compiler_params=params(),
     )(
         doc_lengths,
         first,
         decay_rate,
         step_bias,
-        mixed,
-        rim,
-        rates,
-        conv_weight.reshape(4, 4 * dk),
+        gathered,
+        staged,
+        proj_rates.T,
+        conv_weight,
     )
 
     def joined(late, early):
@@ -290,7 +297,7 @@
         in_specs=[vmem()] * 7,
         out_specs=vmem(),
         compiler_params=params(),
-    )(window, far, follow, own, mixed[:, 4 * dk :], norm_gain.reshape(1, dk), proj_out)
+    )(window, far, follow, own, gate, norm_gain.reshape(1, dk), proj_out)
     shares = lax.all_to_all(share, "tensor", 0, 0, tiled=True)
     return jnp.sum(shares.astype(F32), axis=0).astype(BF16)
 

time: 107 us -> 98.5 us (0.921)
  the two profiles are of different devices: /device:TPU:96 before, /device:TPU:64 now
where the time goes in v2:
time: 98.5 us; the launch traced here: 98.1 us
  blocking collectives  44.2 us (45%)
  starting transfers between devices  29.3 us (30%)
  waiting for transfers between devices  13.7 us (14%)
  Pallas kernels  9.32 us (9%)
    ppermute x6, starting transfers between devices, shifted(): lax.ppermute(array, 'context', [(i, i + by) for i in range(peers - by)])  29.3 us
    all_to_all x1, blocking collectives, local(): gathered = lax.all_to_all(spread, 'tensor', 0, 0, tiled=True)  26.4 us
    all_to_all x1, blocking collectives, local(): shares = lax.all_to_all(share, 'tensor', 0, 0, tiled=True)  17.9 us
    ppermute x6, waiting for transfers between devices, shifted(): lax.ppermute(array, 'context', [(i, i + by) for i in range(peers - by)])  13.7 us
    pallas_call x1, Pallas kernels, local(): pl.pallas_call(chunk_kernel, out_shape=(shape((2, dk, 2 * dk), BF16), sha...  5.92 us
  transfers between devices with their start and end apart: 6, of which 6 were waited for; matrix products, arithmetic and copies ran while one was open for 0% of the time, Pallas kernels for 2%

profile of v2, /device:TPU:64, one launch (start us, length us, event | category | flops | bytes accessed | tf_op | source)
XLA Modules:
  0.0 98.1 jit_solution(8788946236094277110)
XLA Ops:
  0.0 0.7 slice.6
  0.7 1.9 %collective-permute-start = (bf16[16,128]{1,0:T(8,128)(2,1)S(1)}, bf16[16,128]{1,0:T(8,128)(2,1)S(1)}, u32[]{:S(2)}, u32[]{:S(2)}) collective-permute-start(bf16[16,128]{1,0:T(8,128)(2,1)S(1)} %slice.6), channel_id=1, source_target_pairs={{0,1},{1,2},{2,3},{3,4},{4,5},{5,6},{6,7},{7,8},{8,9},{9,10},{10,1... | collective-permute-start | bytes 12296 | tf_op jit(solution)/shard_map/ppermute | solution.py:215
  2.6 0.0 copy-start.1
  2.6 1.9 %shard_map.92.w_ref = bf16[2048,768]{1,0:T(8,128)(2,1)S(1)} custom-call(bf16[2048,768]{1,0:T(8,128)(2,1)} %w_ref.2), custom_call_target="tpu_custom_call" | custom-call | tf_op jit(solution)/shard_map/pallas_call | solution.py:243
  4.6 0.0 copy-start.2
  4.6 0.0 copy-start.3
  4.6 0.0 copy-start.5
  4.6 0.0 copy-start.6
  4.6 0.0 copy-start.7
  4.6 1.0 %collective-permute-done.rim_ref = bf16[16,128]{1,0:T(8,128)(2,1)S(1)} collective-permute-done((bf16[16,128]{1,0:T(8,128)(2,1)S(1)}, bf16[16,128]{1,0:T(8,128)(2,1)S(1)}, u32[]{:S(2)}, u32[]{:S(2)}) %collective-permute-start) | collective-permute-done | bytes 4128 | tf_op jit(solution)/shard_map/ppermute | solution.py:215
  5.6 0.0 copy-done.1
  5.6 0.1 shard_map.91
  5.8 26.4 %all_to_all.10.x_ref = bf16[16,272,128]{2,1,0:T(8,128)(2,1)S(1)} all-to-all(bf16[16,272,128]{2,1,0:T(8,128)(2,1)S(1)} %shard_map.91), channel_id=1, replica_groups=mesh['tensor'=16,'context'=32] {'tensor'}, dimensions={0} | all-to-all | bytes 2228224 | tf_op jit(solution)/shard_map/all_to_all | solution.py:252
  32.1 0.0 copy-done.2
  32.1 0.0 copy-done.3
  32.2 5.9 %shard_map.93 = (bf16[2,128,256]{2,1,0:T(8,128)(2,1)S(1)}, bf16[2,256,128]{2,1,0:T(8,128)(2,1)S(1)}, f32[2,256,128]{2,1,0:T(8,128)S(1)}, bf16[256,256]{1,0:T(8,128)(2,1)S(1)}) custom-call(s32[8]{0:T(128)S(1)} %copy-done.5, s32[1]{0:T(128)} %bitcast.first_ref, f32[2]{0:T(128)S(1)} %copy-done.6, f32[2]{0:T(128)S(1)} %copy-done.7, ...), custom_call_target="tpu_custom_call" | custom-call | tf_op jit(solution)/shard_map/pallas_call | solution.py:254
  38.1 2.6 %collective-permute-start.2 = (bf16[2,128,256]{2,1,0:T(8,128)(2,1)S(1)}, bf16[2,128,256]{2,1,0:T(8,128)(2,1)S(1)}, u32[]{:S(2)}, u32[]{:S(2)}) collective-permute-start(bf16[2,128,256]{2,1,0:T(8,128)(2,1)S(1)} %get-tuple-element.15), channel_id=1, source_target_pairs={{0,2},{1,3},{2,4},{3,5},{4,6},{5,7},{6,8},{7,9},{8,10},{9,11},{10,... | collective-permute-start | bytes 393224 | tf_op jit(solution)/shard_map/ppermute | solution.py:215
  40.7 2.5 %collective-permute-start.1 = (bf16[2,128,256]{2,1,0:T(8,128)(2,1)S(1)}, bf16[2,128,256]{2,1,0:T(8,128)(2,1)S(1)}, u32[]{:S(2)}, u32[]{:S(2)}) collective-permute-start(bf16[2,128,256]{2,1,0:T(8,128)(2,1)S(1)} %get-tuple-element.15), channel_id=1, source_target_pairs={{0,1},{1,2},{2,3},{3,4},{4,5},{5,6},{6,7},{7,8},{8,9},{9,10},{10,1... | collective-permute-start | bytes 393224 | tf_op jit(solution)/shard_map/ppermute | solution.py:215
  43.2 1.9 %collective-permute-done.2.early_ref = bf16[2,128,256]{2,1,0:T(8,128)(2,1)S(1)} collective-permute-done((bf16[2,128,256]{2,1,0:T(8,128)(2,1)S(1)}, bf16[2,128,256]{2,1,0:T(8,128)(2,1)S(1)}, u32[]{:S(2)}, u32[]{:S(2)}) %collective-permute-start.2) | collective-permute-done | bytes 131104 | tf_op jit(solution)/shard_map/ppermute | solution.py:215
  45.0 1.9 %collective-permute-done.1.late_ref = bf16[2,128,256]{2,1,0:T(8,128)(2,1)S(1)} collective-permute-done((bf16[2,128,256]{2,1,0:T(8,128)(2,1)S(1)}, bf16[2,128,256]{2,1,0:T(8,128)(2,1)S(1)}, u32[]{:S(2)}, u32[]{:S(2)}) %collective-permute-start.1) | collective-permute-done | bytes 131104 | tf_op jit(solution)/shard_map/ppermute | solution.py:215
  47.0 0.2 shard_map.94.late_ref
  47.2 5.8 %collective-permute-start.3 = (bf16[2,128,256]{2,1,0:T(8,128)(2,1)S(1)}, bf16[2,128,256]{2,1,0:T(8,128)(2,1)S(1)}, u32[]{:S(2)}, u32[]{:S(2)}) collective-permute-start(bf16[2,128,256]{2,1,0:T(8,128)(2,1)S(1)} %shard_map.94.late_ref), channel_id=1, source_target_pairs={{0,2},{1,3},{2,4},{3,5},{4,6},{5,7},{6,8},{7,9},{8,10},{9,11},{10,... | collective-permute-start | bytes 393224 | tf_op jit(solution)/shard_map/ppermute | solution.py:215
  53.0 2.9 %collective-permute-done.3.early_ref = bf16[2,128,256]{2,1,0:T(8,128)(2,1)S(1)} collective-permute-done((bf16[2,128,256]{2,1,0:T(8,128)(2,1)S(1)}, bf16[2,128,256]{2,1,0:T(8,128)(2,1)S(1)}, u32[]{:S(2)}, u32[]{:S(2)}) %collective-permute-start.3) | collective-permute-done | bytes 131104 | tf_op jit(solution)/shard_map/ppermute | solution.py:215
  55.9 0.2 shard_map.95.late_ref
  56.1 8.1 %collective-permute-start.4 = (bf16[2,128,256]{2,1,0:T(8,128)(2,1)S(1)}, bf16[2,128,256]{2,1,0:T(8,128)(2,1)S(1)}, u32[]{:S(2)}, u32[]{:S(2)}) collective-permute-start(bf16[2,128,256]{2,1,0:T(8,128)(2,1)S(1)} %shard_map.95.late_ref), channel_id=1, source_target_pairs={{0,4},{1,5},{2,6},{3,7},{4,8},{5,9},{6,10},{7,11},{8,12},{9,13},{1... | collective-permute-start | bytes 393224 | tf_op jit(solution)/shard_map/ppermute | solution.py:215
  64.2 2.8 %collective-permute-done.4.early_ref = bf16[2,128,256]{2,1,0:T(8,128)(2,1)S(1)} collective-permute-done((bf16[2,128,256]{2,1,0:T(8,128)(2,1)S(1)}, bf16[2,128,256]{2,1,0:T(8,128)(2,1)S(1)}, u32[]{:S(2)}, u32[]{:S(2)}) %collective-permute-start.4) | collective-permute-done | bytes 131104 | tf_op jit(solution)/shard_map/ppermute | solution.py:215
  67.0 0.2 shard_map.96.near_ref
  67.2 8.3 %collective-permute-start.5 = (bf16[2,128,128]{2,1,0:T(8,128)(2,1)S(1)}, bf16[2,128,128]{2,1,0:T(8,128)(2,1)S(1)}, u32[]{:S(2)}, u32[]{:S(2)}) collective-permute-start(bf16[2,128,128]{2,1,0:T(8,128)(2,1)S(1)} %slice.8), channel_id=1, source_target_pairs={{0,8},{1,9},{2,10},{3,11},{4,12},{5,13},{6,14},{7,15},{8,16},{9,17... | collective-permute-start | bytes 196616 | tf_op jit(solution)/shard_map/ppermute | solution.py:215
  75.5 3.2 %collective-permute-done.5.far_ref = bf16[2,128,128]{2,1,0:T(8,128)(2,1)S(1)} collective-permute-done((bf16[2,128,128]{2,1,0:T(8,128)(2,1)S(1)}, bf16[2,128,128]{2,1,0:T(8,128)(2,1)S(1)}, u32[]{:S(2)}, u32[]{:S(2)}) %collective-permute-start.5) | collective-permute-done | bytes 65568 | tf_op jit(solution)/shard_map/ppermute | solution.py:215
  78.7 0.8 shard_map.97
  79.5 17.9 %all_to_all.11 = bf16[16,256,128]{2,1,0:T(8,128)(2,1)S(1)} all-to-all(bf16[16,256,128]{2,1,0:T(8,128)(2,1)S(1)} %shard_map.97), channel_id=1, replica_groups=mesh['tensor'=16,'context'=32] {'tensor'}, dimensions={0} | all-to-all | bytes 2097152 | tf_op jit(solution)/shard_map/all_to_all | solution.py:301
  97.4 0.8 reduce_sum.12
  (8 shorter events, 0.0 us)
Async XLA Ops:
  0.7 4.9 %collective-permute-start = (bf16[16,128]{1,0:T(8,128)(2,1)S(1)}, bf16[16,128]{1,0:T(8,128)(2,1)S(1)}, u32[]{:S(2)}, u32[]{:S(2)}) collective-permute-start(bf16[16,128]{1,0:T(8,128)(2,1)S(1)} %slice.6), channel_id=1, source_target_pairs={{0,1},{1,2},{2,3},{3,4},{4,5},{5,6},{6,7},{7,8},{8,9},{9,10},{10,1... | collective-permute-start | bytes 12296 | tf_op jit(solution)/shard_map/ppermute | solution.py:215
  2.6 3.0 %copy-start.1 = (bf16[256,128]{1,0:T(8,128)(2,1)S(1)}, bf16[256,128]{1,0:T(8,128)(2,1)}, u32[]{:S(2)}) copy-start(bf16[256,128]{1,0:T(8,128)(2,1)} %x_ref.1) | copy-start | bytes 196612
  4.6 27.6 %copy-start.2 = (bf16[2048,4]{0,1:T(4,128)(2,1)S(1)}, bf16[2048,4]{0,1:T(4,128)(2,1)}, u32[]{:S(2)}) copy-start(bf16[2048,4]{0,1:T(4,128)(2,1)} %param.11) | copy-start | bytes 49156
  4.6 27.6 %copy-start.3 = (f32[4,1,512]{2,1,0:T(1,128)S(1)}, f32[4,1,512]{2,1,0:T(1,128)}, u32[]{:S(2)}) copy-start(f32[4,1,512]{2,1,0:T(1,128)} %cw_ref.1) | copy-start | bytes 24580
  4.6 27.5 %copy-start.5 = (s32[8]{0:T(128)S(1)}, s32[8]{0:T(128)}, u32[]{:S(2)}) copy-start(s32[8]{0:T(128)} %lens_ref.1) | copy-start | bytes 100
  4.6 27.5 %copy-start.6 = (f32[2]{0:T(128)S(1)}, f32[2]{0:T(128)}, u32[]{:S(2)}) copy-start(f32[2]{0:T(128)} %rate_ref.1) | copy-start | bytes 28
  4.6 27.5 %copy-start.7 = (f32[2]{0:T(128)S(1)}, f32[2]{0:T(128)}, u32[]{:S(2)}) copy-start(f32[2]{0:T(128)} %bias_ref.1) | copy-start | bytes 28
  32.1 46.6 %copy-start = (bf16[256,2048]{1,0:T(8,128)(2,1)S(1)}, bf16[256,2048]{1,0:T(8,128)(2,1)}, u32[]{:S(2)}) copy-start(bf16[256,2048]{1,0:T(8,128)(2,1)} %w_ref.3) | copy-start | bytes 3145732
  32.1 46.6 %copy-start.4 = (f32[128]{0:T(128)S(1)}, f32[128]{0:T(128)}, u32[]{:S(2)}) copy-start(f32[128]{0:T(128)} %param.15) | copy-start | bytes 1540
  38.1 7.0 %collective-permute-start.2 = (bf16[2,128,256]{2,1,0:T(8,128)(2,1)S(1)}, bf16[2,128,256]{2,1,0:T(8,128)(2,1)S(1)}, u32[]{:S(2)}, u32[]{:S(2)}) collective-permute-start(bf16[2,128,256]{2,1,0:T(8,128)(2,1)S(1)} %get-tuple-element.15), channel_id=1, source_target_pairs={{0,2},{1,3},{2,4},{3,5},{4,6},{5,7},{6,8},{7,9},{8,10},{9,11},{10,... | collective-permute-start | bytes 393224 | tf_op jit(solution)/shard_map/ppermute | solution.py:215
  40.7 6.3 %collective-permute-start.1 = (bf16[2,128,256]{2,1,0:T(8,128)(2,1)S(1)}, bf16[2,128,256]{2,1,0:T(8,128)(2,1)S(1)}, u32[]{:S(2)}, u32[]{:S(2)}) collective-permute-start(bf16[2,128,256]{2,1,0:T(8,128)(2,1)S(1)} %get-tuple-element.15), channel_id=1, source_target_pairs={{0,1},{1,2},{2,3},{3,4},{4,5},{5,6},{6,7},{7,8},{8,9},{9,10},{10,1... | collective-permute-start | bytes 393224 | tf_op jit(solution)/shard_map/ppermute | solution.py:215
  47.2 8.7 %collective-permute-start.3 = (bf16[2,128,256]{2,1,0:T(8,128)(2,1)S(1)}, bf16[2,128,256]{2,1,0:T(8,128)(2,1)S(1)}, u32[]{:S(2)}, u32[]{:S(2)}) collective-permute-start(bf16[2,128,256]{2,1,0:T(8,128)(2,1)S(1)} %shard_map.94.late_ref), channel_id=1, source_target_pairs={{0,2},{1,3},{2,4},{3,5},{4,6},{5,7},{6,8},{7,9},{8,10},{9,11},{10,... | collective-permute-start | bytes 393224 | tf_op jit(solution)/shard_map/ppermute | solution.py:215
  56.1 10.9 %collective-permute-start.4 = (bf16[2,128,256]{2,1,0:T(8,128)(2,1)S(1)}, bf16[2,128,256]{2,1,0:T(8,128)(2,1)S(1)}, u32[]{:S(2)}, u32[]{:S(2)}) collective-permute-start(bf16[2,128,256]{2,1,0:T(8,128)(2,1)S(1)} %shard_map.95.late_ref), channel_id=1, source_target_pairs={{0,4},{1,5},{2,6},{3,7},{4,8},{5,9},{6,10},{7,11},{8,12},{9,13},{1... | collective-permute-start | bytes 393224 | tf_op jit(solution)/shard_map/ppermute | solution.py:215
  67.2 11.5 %collective-permute-start.5 = (bf16[2,128,128]{2,1,0:T(8,128)(2,1)S(1)}, bf16[2,128,128]{2,1,0:T(8,128)(2,1)S(1)}, u32[]{:S(2)}, u32[]{:S(2)}) collective-permute-start(bf16[2,128,128]{2,1,0:T(8,128)(2,1)S(1)} %slice.8), channel_id=1, source_target_pairs={{0,8},{1,9},{2,10},{3,11},{4,12},{5,13},{6,14},{7,15},{8,16},{9,17... | collective-permute-start | bytes 196616 | tf_op jit(solution)/shard_map/ppermute | solution.py:215

commit v3 on v2

--- a/solution.py
+++ b/solution.py
@@ -46,16 +46,16 @@
     rows = lowers[0].shape[0]
     eye = (rows_at == cols_at).astype(F32)
 
-    def between(lower, size):
-        joins = ((rows_at // (2 * size)) == (cols_at // (2 * size))) & (
-            (rows_at // size) != (cols_at // size)
-        )
-        return jnp.where(joins, lower, 0.0)
-
-    found = [eye - between(lower, 1) for lower in lowers]
+    def joins(size):
+        together = (rows_at // (2 * size)) == (cols_at // (2 * size))
+        return together & ((rows_at // size) != (cols_at // size))
+
+    first = joins(1)
+    found = [eye - jnp.where(first, lower, 0.0) for lower in lowers]
     size = 2
     while size < rows:
-        halfway = [mm(between(lower, size), t) for lower, t in zip(lowers, found)]
+        mask = joins(size)
+        halfway = [mm(jnp.where(mask, lower, 0.0), t) for lower, t in zip(lowers, found)]
         found = [t - mm(t, h) for t, h in zip(found, halfway)]
         size *= 2
     return found
@@ -71,9 +71,11 @@
     wr_ref,
     cw_ref,
     c_ref,
-    m_ref,
-    o_ref,
-    z_ref,
+    wu_ref,
+    ratio_ref,
+    q_ref,
+    k_ref,
+    follow_ref,
     wide,
     ext,
 ):
@@ -82,9 +84,8 @@
     dk = cw_ref.shape[2] // 4
     for part in range(parts):
         wide[:, part * width : (part + 1) * width] = x_ref[part]
-    mixed = jnp.dot(wide[...], w_ref[...], preferred_element_type=F32)
-    ext[...] = mixed[:, : 4 * dk].astype(BF16).astype(F32)
-    z_ref[...] = mixed[TAIL : TAIL + rows, 4 * dk :].astype(BF16)
+    mixed = jnp.dot(wide[...], w_ref[:, : 4 * dk], preferred_element_type=F32)
+    ext[...] = mixed.astype(BF16).astype(F32)
     rates = mm_nt(wide[TAIL : TAIL + rows, :], wr_ref[...]).astype(BF16).astype(F32)
     first = first_ref[0]
     pos = first + lax.broadcasted_iota(jnp.int32, (rows, 1), 0)
@@ -132,40 +133,66 @@
 
     visible = lower & (cols_at + first >= start)
     gram = mm_nt(kb, kb)
-    cross = mm_nt(qb, kb)
     last_start = start[rows - 1 : rows, :]
     carries = (start < first).astype(F32)
     in_tail = (pos >= last_start).astype(F32)
-
-    lowers, scores = [], []
-    for h in range(2):
-        differ = cumul[:, h : h + 1] - cumul_t[h : h + 1, :]
-        ratio = jnp.where(visible, jnp.exp(jnp.where(visible, differ, 0.0)), 0.0)
-        scores.append(cross * ratio)
-        lowers.append(
-            jnp.where(rows_at > cols_at, betas[:, h : h + 1] * ratio * gram, 0.0)
-        )
-    inverses = unit_lower_inverses(lowers, rows_at, cols_at)
-    square = lax.broadcasted_iota(jnp.int32, (dk, 2 * dk), 0)
-    across = lax.broadcasted_iota(jnp.int32, (dk, 2 * dk), 1)
+    q_ref[...] = qb
+    k_ref[...] = kb
+
+    half = rows // 2
+    diagonals, below, rights = [], [], []
     for h in range(2):
         col = cumul[:, h : h + 1]
         beta = betas[:, h : h + 1]
         gamma = jnp.exp(col) * carries
+        differ = col - cumul_t[h : h + 1, :]
+        ratio = jnp.where(visible, jnp.exp(jnp.where(visible, differ, 0.0)), 0.0)
+        ratio_ref[h] = ratio
+        weighed = beta * ratio * gram
+        diagonals.append(weighed[:half, :half])
+        diagonals.append(weighed[half:, half:])
+        below.append(weighed[half:, :half])
         value = conv[:, (2 + h) * dk : (3 + h) * dk]
-        rhs = jnp.concatenate([(beta * gamma) * k, beta * value], axis=1)
-        wu = mm(inverses[h], rhs)
+        rights.append(jnp.concatenate([(beta * gamma) * k, beta * value], axis=1))
+        follow_ref[h] = (gamma * q).astype(BF16)
+    inverses = unit_lower_inverses(
+        diagonals, rows_at[:half, :half], cols_at[:half, :half]
+    )
+    tops = [mm(inverses[2 * h], rights[h][:half]) for h in range(2)]
+    reduced = [rights[h][half:] - mm(below[h], tops[h]) for h in range(2)]
+    bottoms = [mm(inverses[2 * h + 1], reduced[h]) for h in range(2)]
+    square = lax.broadcasted_iota(jnp.int32, (dk, 2 * dk), 0)
+    across = lax.broadcasted_iota(jnp.int32, (dk, 2 * dk), 1)
+    for h in range(2):
+        col = cumul[:, h : h + 1]
         last = col[rows - 1 : rows, :]
-        tail = jnp.exp(last - col) * in_tail
-        k_tail = jnp.transpose(k * tail)
-        made = mm(k_tail, wu)
-        gamma_last = gamma[rows - 1 : rows, :]
+        k_tail = jnp.transpose(k * (jnp.exp(last - col) * in_tail)).astype(BF16)
+        wu = jnp.concatenate([tops[h], bottoms[h]], axis=0).astype(BF16)
+        wu_ref[h] = wu
+        made = jnp.dot(k_tail, wu, preferred_element_type=F32)
+        gamma_last = jnp.exp(last) * carries[rows - 1 : rows, :]
         c_ref[h] = (
             jnp.where(square == across, gamma_last, 0.0) + jnp.where(across < dk, -made, made)
         ).astype(BF16)
-        both = mm(scores[h], wu)
-        m_ref[h] = (gamma * q - both[:, :dk]).astype(BF16)
+
+
+def detail_kernel(
+    x_ref, w_ref, wu_ref, ratio_ref, q_ref, k_ref, follow_ref, gain_ref, m_ref, o_ref, gate_ref, wide
+):
+    parts, rows, width = x_ref.shape
+    rows = rows - TAIL
+    dk = gain_ref.shape[1]
+    cross = mm_nt(q_ref[...], k_ref[...])
+    for h in range(2):
+        both = mm(cross * ratio_ref[h], wu_ref[h])
+        m_ref[h] = (follow_ref[h].astype(F32) - both[:, :dk]).astype(BF16)
         o_ref[h] = both[:, dk:]
+    for part in range(parts):
+        wide[:, part * width : (part + 1) * width] = x_ref[part, TAIL : TAIL + rows, :]
+    z = jnp.dot(wide[...], w_ref[:, 4 * dk :], preferred_element_type=F32)
+    gate = silu(z.astype(BF16).astype(F32))
+    for h in range(2):
+        gate_ref[:, h * dk : (h + 1) * dk] = gate[:, h * dk : (h + 1) * dk] * gain_ref[...]
 
 
 def compose(late, early):
@@ -180,18 +207,28 @@
         out_ref[h] = compose(late_ref[h], early_ref[h]).astype(BF16)
 
 
-def finish_kernel(near_ref, far_ref, m_ref, o_ref, gate_ref, gain_ref, w_ref, out_ref):
-    dk = gain_ref.shape[1]
+def advance(summary, state):
+    dk = summary.shape[0]
+    moved = jnp.dot(summary[:, :dk], state, preferred_element_type=F32)
+    return (moved + summary[:, dk:].astype(F32)).astype(BF16)
+
+
+def enter_kernel(near_ref, far_ref, out_ref):
+    for h in range(2):
+        out_ref[h] = advance(near_ref[h], far_ref[h])
+
+
+def finish_kernel(
+    made_ref, given_ref, first_half_ref, m_ref, o_ref, gate_ref, w_ref, out_ref
+):
+    dk = m_ref.shape[2]
     parts, _, width = out_ref.shape
     sides = []
     for h in range(2):
-        near = near_ref[h]
-        state = jnp.dot(near[:, :dk], far_ref[h], preferred_element_type=F32)
-        state = state + near[:, dk:].astype(F32)
-        rec = o_ref[h] + jnp.dot(m_ref[h], state.astype(BF16), preferred_element_type=F32)
+        state = given_ref[h] + advance(first_half_ref[h], made_ref[h])
+        rec = o_ref[h] + jnp.dot(m_ref[h], state, preferred_element_type=F32)
         scale = lax.rsqrt(jnp.mean(rec * rec, -1, keepdims=True) + 1e-6)
-        gate = silu(gate_ref[:, h * dk : (h + 1) * dk].astype(F32))
-        sides.append((rec * scale * gain_ref[...] * gate).astype(BF16))
+        sides.append((rec * scale * gate_ref[:, h * dk : (h + 1) * dk]).astype(BF16))
     normed = jnp.concatenate(sides, axis=1)
     share = jnp.dot(normed, w_ref[...], preferred_element_type=F32).astype(BF16)
     for part in range(parts):
@@ -213,6 +250,18 @@
 def shifted(array, by):
     peers = lax.axis_size("context")
     return lax.ppermute(array, "context", [(i, i + by) for i in range(peers - by)])
+
+
+def within_chip(array, source):
+    peers = lax.axis_size("context")
+    pairs = [(i + source, i + 1 - source) for i in range(0, peers, 2)]
+    return lax.ppermute(array, "context", pairs)
+
+
+def over_chips(array, by):
+    peers = lax.axis_size("context")
+    pairs = [(i, i + 2 * by) for i in range(1, peers - 2 * by, 2)]
+    return lax.ppermute(array, "context", pairs)
 
 
 def local(
@@ -251,16 +300,18 @@
     spread, staged, first = lax.optimization_barrier((spread, staged, first))
     gathered = lax.all_to_all(spread, "tensor", 0, 0, tiled=True)
 
-    summary, follow, own, gate = pl.pallas_call(
+    summary, inner, ratio, query, key, reach = pl.pallas_call(
         chunk_kernel,
         out_shape=(
             shape((2, dk, 2 * dk), BF16),
+            shape((2, rows, 2 * dk), BF16),
+            shape((2, rows, rows), F32),
+            shape((rows, dk), BF16),
+            shape((rows, dk), BF16),
             shape((2, rows, dk), BF16),
-            shape((2, rows, dk), F32),
-            shape((rows, 2 * dk), BF16),
         ),
         in_specs=[smem()] * 4 + [vmem()] * 4,
-        out_specs=(vmem(),) * 4,
+        out_specs=(vmem(),) * 6,
         scratch_shapes=[
             pltpu.VMEM((rows + TAIL, peers * width), BF16),
             pltpu.VMEM((rows + TAIL, 4 * dk), F32),
@@ -276,20 +327,35 @@
         proj_rates.T,
         conv_weight,
     )
-
-    def joined(late, early):
+    follow, own, gate = pl.pallas_call(
+        detail_kernel,
+        out_shape=(
+            shape((2, rows, dk), BF16),
+            shape((2, rows, dk), F32),
+            shape((rows, 2 * dk), F32),
+        ),
+        in_specs=[vmem()] * 8,
+        out_specs=(vmem(),) * 3,
+        scratch_shapes=[pltpu.VMEM((rows, peers * width), BF16)],
+        compiler_params=params(),
+    )(gathered, staged, inner, ratio, query, key, reach, norm_gain.reshape(1, dk))
+
+    def small(kernel, columns, *arrays):
         return pl.pallas_call(
-            compose_kernel,
-            out_shape=shape((2, dk, 2 * dk), BF16),
-            in_specs=[vmem()] * 2,
+            kernel,
+            out_shape=shape((2, dk, columns), BF16),
+            in_specs=[vmem()] * len(arrays),
             out_specs=vmem(),
             compiler_params=params(),
-        )(late, early)
-
-    window = joined(shifted(summary, 1), shifted(summary, 2))
-    window = joined(window, shifted(window, 2))
-    window = joined(window, shifted(window, 4))
-    far = shifted(window[:, :, dk:], 8)
+        )(*arrays)
+
+    first_half = within_chip(summary, 0)
+    first_half, follow, own, gate = lax.optimization_barrier((first_half, follow, own, gate))
+    chip = small(compose_kernel, 2 * dk, summary, first_half)
+    window = small(compose_kernel, 2 * dk, over_chips(chip, 1), over_chips(chip, 2))
+    window = small(compose_kernel, 2 * dk, window, over_chips(window, 2))
+    made = small(enter_kernel, dk, window, over_chips(window[:, :, dk:], 4))
+    given = within_chip(made, 1)
 
     share = pl.pallas_call(
         finish_kernel,
@@ -297,7 +363,7 @@
         in_specs=[vmem()] * 7,
         out_specs=vmem(),
         compiler_params=params(),
-    )(window, far, follow, own, gate, norm_gain.reshape(1, dk), proj_out)
+    )(made, given, first_half, follow, own, gate, proj_out)
     shares = lax.all_to_all(share, "tensor", 0, 0, tiled=True)
     return jnp.sum(shares.astype(F32), axis=0).astype(BF16)
 

time: 98.5 us -> 95.7 us (0.972)
  the two profiles are of different devices: /device:TPU:64 before, /device:TPU:32 now
where the time goes in v3:
time: 95.7 us; the launch traced here: 95.3 us
  blocking collectives  47 us (49%)
  waiting for transfers between devices  30.1 us (31%)
  Pallas kernels  9.06 us (9%)
  starting transfers between devices  7.45 us (8%)
    ppermute x2, waiting for transfers between devices, within_chip(): return lax.ppermute(array, 'context', pairs)  29.1 us
    all_to_all x1, blocking collectives, local(): gathered = lax.all_to_all(spread, 'tensor', 0, 0, tiled=True)  26.4 us
    all_to_all x1, blocking collectives, local(): shares = lax.all_to_all(share, 'tensor', 0, 0, tiled=True)  20.6 us
    pallas_call x1, Pallas kernels, local(): pl.pallas_call(chunk_kernel, out_shape=(shape((2, dk, 2 * dk), BF16), sha...  4.86 us
    ppermute x2, starting transfers between devices, within_chip(): return lax.ppermute(array, 'context', pairs)  2.87 us
    ppermute x4, starting transfers between devices, over_chips(): return lax.ppermute(array, 'context', pairs)  2.67 us
    pallas_call x1, Pallas kernels, local(): pl.pallas_call(stage_kernel, out_shape=shape(proj_qkvz.shape, BF16), in_s...  1.93 us
  transfers between devices with their start and end apart: 7, of which 3 were waited for; matrix products, arithmetic and copies ran while one was open for 0% of the time, Pallas kernels for 3%

profile of v3, /device:TPU:32, one launch (start us, length us, event | category | flops | bytes accessed | tf_op | source)
XLA Modules:
  0.0 95.3 jit_solution(2430927961847109166)
XLA Ops:
  0.0 0.7 slice.6
  0.7 1.9 %collective-permute-start = (bf16[16,128]{1,0:T(8,128)(2,1)S(1)}, bf16[16,128]{1,0:T(8,128)(2,1)S(1)}, u32[]{:S(2)}, u32[]{:S(2)}) collective-permute-start(bf16[16,128]{1,0:T(8,128)(2,1)S(1)} %slice.6), channel_id=1, source_target_pairs={{0,1},{1,2},{2,3},{3,4},{4,5},{5,6},{6,7},{7,8},{8,9},{9,10},{10,1... | collective-permute-start | bytes 12296 | tf_op jit(solution)/shard_map/ppermute | solution.py:252
  2.6 0.0 copy-start.1
  2.6 1.9 %shard_map.92.w_ref = bf16[2048,768]{1,0:T(8,128)(2,1)S(1)} custom-call(bf16[2048,768]{1,0:T(8,128)(2,1)} %w_ref.2), custom_call_target="tpu_custom_call" | custom-call | tf_op jit(solution)/shard_map/pallas_call | solution.py:292
  4.6 0.0 copy-start.2
  4.6 0.0 copy-start.3
  4.6 0.0 copy-start.5
  4.6 0.0 copy-start.6
  4.6 0.0 copy-start.7
  4.6 1.0 %collective-permute-done.rim_ref = bf16[16,128]{1,0:T(8,128)(2,1)S(1)} collective-permute-done((bf16[16,128]{1,0:T(8,128)(2,1)S(1)}, bf16[16,128]{1,0:T(8,128)(2,1)S(1)}, u32[]{:S(2)}, u32[]{:S(2)}) %collective-permute-start) | collective-permute-done | bytes 4128 | tf_op jit(solution)/shard_map/ppermute | solution.py:252
  5.6 0.1 shard_map.91
  5.8 0.0 copy-start.4
  5.8 26.4 %all_to_all.10.x_ref = bf16[16,272,128]{2,1,0:T(8,128)(2,1)S(1)} all-to-all(bf16[16,272,128]{2,1,0:T(8,128)(2,1)S(1)} %shard_map.91), channel_id=1, replica_groups=mesh['tensor'=16,'context'=32] {'tensor'}, dimensions={0} | all-to-all | bytes 2228224 | tf_op jit(solution)/shard_map/all_to_all | solution.py:301
  32.2 4.9 %shard_map.93 = (bf16[2,128,256]{2,1,0:T(8,128)(2,1)S(1)}, bf16[2,256,256]{2,1,0:T(8,128)(2,1)S(1)}, f32[2,256,256]{2,1,0:T(8,128)S(1)}, bf16[256,128]{1,0:T(8,1...) custom-call(s32[8]{0:T(128)S(1)} %copy-done.5, s32[1]{0:T(128)} %bitcast.first_ref, ...), custom_call_target="tpu_custom_call" | custom-call | tf_op jit(solution)/shard_map/pallas_call | solution.py:303
  37.0 1.6 %collective-permute-start.1 = (bf16[2,128,256]{2,1,0:T(8,128)(2,1)S(1)}, bf16[2,128,256]{2,1,0:T(8,128)(2,1)S(1)}, u32[]{:S(2)}, u32[]{:S(2)}) collective-permute-start(bf16[2,128,256]{2,1,0:T(8,128)(2,1)S(1)} %get-tuple-element.24.late_ref), channel_id=1, source_target_pairs={{0,1},{2,3},{4,5},{6,7},{8,9},{10,11},{12,13},{14,15},{16,17},{18,... | collective-permute-start | bytes 393224 | tf_op jit(solution)/shard_map/ppermute | solution.py:258
  38.6 0.0 copy-start
  38.6 0.7 shard_map.94
  39.3 0.3 collective-permute-done.1.early_ref.first_half_ref
  39.6 0.2 shard_map.95
  39.8 0.7 collective-permute-start.3
  40.4 0.7 collective-permute-start.2
  41.1 0.0 collective-permute-done.3.early_ref
  41.1 0.2 shard_map.96.late_ref
  41.3 0.7 collective-permute-start.4
  42.0 0.2 shard_map.97.near_ref
  42.2 0.7 collective-permute-start.5
  42.9 0.2 shard_map.98.made_ref
  43.0 1.3 %collective-permute-start.6 = (bf16[2,128,128]{2,1,0:T(8,128)(2,1)S(1)}, bf16[2,128,128]{2,1,0:T(8,128)(2,1)S(1)}, u32[]{:S(2)}, u32[]{:S(2)}) collective-permute-start(bf16[2,128,128]{2,1,0:T(8,128)(2,1)S(1)} %shard_map.98.made_ref), channel_id=1, source_target_pairs={{1,0},{3,2},{5,4},{7,6},{9,8},{11,10},{13,12},{15,14},{17,16},{19,... | collective-permute-start | bytes 196616 | tf_op jit(solution)/shard_map/ppermute | solution.py:258
  44.3 28.8 %collective-permute-done.6.given_ref = bf16[2,128,128]{2,1,0:T(8,128)(2,1)S(1)} collective-permute-done((bf16[2,128,128]{2,1,0:T(8,128)(2,1)S(1)}, bf16[2,128,128]{2,1,0:T(8,128)(2,1)S(1)}, u32[]{:S(2)}, u32[]{:S(2)}) %collective-permute-start.6) | collective-permute-done | bytes 65568 | tf_op jit(solution)/shard_map/ppermute | solution.py:258
  73.1 0.8 shard_map.99
  73.9 20.6 %all_to_all.11 = bf16[16,256,128]{2,1,0:T(8,128)(2,1)S(1)} all-to-all(bf16[16,256,128]{2,1,0:T(8,128)(2,1)S(1)} %shard_map.99), channel_id=1, replica_groups=mesh['tensor'=16,'context'=32] {'tensor'}, dimensions={0} | all-to-all | bytes 2097152 | tf_op jit(solution)/shard_map/all_to_all | solution.py:367
  94.5 0.8 reduce_sum.12
  (12 shorter events, 0.0 us)
Async XLA Ops:
  0.7 4.9 %collective-permute-start = (bf16[16,128]{1,0:T(8,128)(2,1)S(1)}, bf16[16,128]{1,0:T(8,128)(2,1)S(1)}, u32[]{:S(2)}, u32[]{:S(2)}) collective-permute-start(bf16[16,128]{1,0:T(8,128)(2,1)S(1)} %slice.6), channel_id=1, source_target_pairs={{0,1},{1,2},{2,3},{3,4},{4,5},{5,6},{6,7},{7,8},{8,9},{9,10},{10,1... | collective-permute-start | bytes 12296 | tf_op jit(solution)/shard_map/ppermute | solution.py:252
  2.6 3.0 %copy-start.1 = (bf16[256,128]{1,0:T(8,128)(2,1)S(1)}, bf16[256,128]{1,0:T(8,128)(2,1)}, u32[]{:S(2)}) copy-start(bf16[256,128]{1,0:T(8,128)(2,1)} %x_ref.1) | copy-start | bytes 196612
  4.6 27.6 %copy-start.2 = (bf16[2048,4]{0,1:T(4,128)(2,1)S(1)}, bf16[2048,4]{0,1:T(4,128)(2,1)}, u32[]{:S(2)}) copy-start(bf16[2048,4]{0,1:T(4,128)(2,1)} %param.11) | copy-start | bytes 49156
  4.6 27.6 %copy-start.3 = (f32[4,1,512]{2,1,0:T(1,128)S(1)}, f32[4,1,512]{2,1,0:T(1,128)}, u32[]{:S(2)}) copy-start(f32[4,1,512]{2,1,0:T(1,128)} %cw_ref.1) | copy-start | bytes 24580
  4.6 27.5 %copy-start.5 = (s32[8]{0:T(128)S(1)}, s32[8]{0:T(128)}, u32[]{:S(2)}) copy-start(s32[8]{0:T(128)} %lens_ref.1) | copy-start | bytes 100
  4.6 27.5 %copy-start.6 = (f32[2]{0:T(128)S(1)}, f32[2]{0:T(128)}, u32[]{:S(2)}) copy-start(f32[2]{0:T(128)} %rate_ref.1) | copy-start | bytes 28
  4.6 27.5 %copy-start.7 = (f32[2]{0:T(128)S(1)}, f32[2]{0:T(128)}, u32[]{:S(2)}) copy-start(f32[2]{0:T(128)} %bias_ref.1) | copy-start | bytes 28
  5.8 32.9 %copy-start.4 = (f32[128]{0:T(128)S(1)}, f32[128]{0:T(128)}, u32[]{:S(2)}) copy-start(f32[128]{0:T(128)} %param.15) | copy-start | bytes 1540
  37.0 2.5 %collective-permute-start.1 = (bf16[2,128,256]{2,1,0:T(8,128)(2,1)S(1)}, bf16[2,128,256]{2,1,0:T(8,128)(2,1)S(1)}, u32[]{:S(2)}, u32[]{:S(2)}) collective-permute-start(bf16[2,128,256]{2,1,0:T(8,128)(2,1)S(1)} %get-tuple-element.24.late_ref), channel_id=1, source_target_pairs={{0,1},{2,3},{4,5},{6,7},{8,9},{10,11},{12,13},{14,15},{16,17},{18,... | collective-permute-start | bytes 393224 | tf_op jit(solution)/shard_map/ppermute | solution.py:258
  38.6 34.5 %copy-start = (bf16[256,2048]{1,0:T(8,128)(2,1)S(1)}, bf16[256,2048]{1,0:T(8,128)(2,1)}, u32[]{:S(2)}) copy-start(bf16[256,2048]{1,0:T(8,128)(2,1)} %w_ref.3) | copy-start | bytes 3145732
  39.8 1.4 %collective-permute-start.3 = (bf16[2,128,256]{2,1,0:T(8,128)(2,1)S(1)}, bf16[2,128,256]{2,1,0:T(8,128)(2,1)S(1)}, u32[]{:S(2)}, u32[]{:S(2)}) collective-permute-start(bf16[2,128,256]{2,1,0:T(8,128)(2,1)S(1)} %shard_map.95), channel_id=1, source_target_pairs={{1,5},{3,7},{5,9},{7,11},{9,13},{11,15},{13,17},{15,19},{17,21},{1... | collective-permute-start | bytes 393224 | tf_op jit(solution)/shard_map/ppermute | solution.py:264
  40.4 0.7 collective-permute-start.2
  41.3 0.7 collective-permute-start.4
  42.2 0.7 collective-permute-start.5
  43.0 30.1 %collective-permute-start.6 = (bf16[2,128,128]{2,1,0:T(8,128)(2,1)S(1)}, bf16[2,128,128]{2,1,0:T(8,128)(2,1)S(1)}, u32[]{:S(2)}, u32[]{:S(2)}) collective-permute-start(bf16[2,128,128]{2,1,0:T(8,128)(2,1)S(1)} %shard_map.98.made_ref), channel_id=1, source_target_pairs={{1,0},{3,2},{5,4},{7,6},{9,8},{11,10},{13,12},{15,14},{17,16},{19,... | collective-permute-start | bytes 196616 | tf_op jit(solution)/shard_map/ppermute | solution.py:258

commit v4 on v3

--- a/solution.py
+++ b/solution.py
@@ -30,7 +30,7 @@
 
 def spread_kernel(x_ref, rim_ref, out_ref):
     block = x_ref[...]
-    rim = rim_ref[...]
+    rim = rim_ref[rim_ref.shape[0] - TAIL :, :]
     for part in range(out_ref.shape[0]):
         out_ref[part, 0:TAIL, :] = rim
         out_ref[part, TAIL:, :] = block
@@ -46,9 +46,10 @@
     rows = lowers[0].shape[0]
     eye = (rows_at == cols_at).astype(F32)
 
+    apart = rows_at ^ cols_at
+
     def joins(size):
-        together = (rows_at // (2 * size)) == (cols_at // (2 * size))
-        return together & ((rows_at // size) != (cols_at // size))
+        return (apart >= size) & (apart < 2 * size)
 
     first = joins(1)
     found = [eye - jnp.where(first, lower, 0.0) for lower in lowers]
@@ -281,7 +282,7 @@
     first = (lax.axis_index("context") * rows).astype(jnp.int32).reshape(1)
     shape = jax.ShapeDtypeStruct
 
-    tail = shifted(hidden[rows - TAIL :], 1)
+    tail = shifted(hidden, 1)
     spread = pl.pallas_call(
         spread_kernel,
         out_shape=shape((peers, TAIL + rows, width), BF16),

time: 95.7 us -> 95.3 us (level)
  waiting for transfers between devices: 30.1 us -> 32 us
  blocking collectives: 47 us -> 45.7 us
    all_to_all x1, blocking collectives: 26.4 us -> 25.1 us  [local(): gathered = lax.all_to_all(spread, 'tensor', 0, 0, tiled=True)]
    ppermute x2, waiting for transfers between devices: 29.1 us -> 30.1 us  [within_chip(): return lax.ppermute(array, 'context', pairs)]
where the time goes in v4:
time: 95.3 us; the launch traced here: 95 us
  blocking collectives  45.7 us (48%)
  waiting for transfers between devices  32 us (34%)
  Pallas kernels  9.04 us (9%)
  starting transfers between devices  7.17 us (8%)
    ppermute x2, waiting for transfers between devices, within_chip(): return lax.ppermute(array, 'context', pairs)  30.1 us
    all_to_all x1, blocking collectives, local(): gathered = lax.all_to_all(spread, 'tensor', 0, 0, tiled=True)  25.1 us
    all_to_all x1, blocking collectives, local(): shares = lax.all_to_all(share, 'tensor', 0, 0, tiled=True)  20.6 us
    pallas_call x1, Pallas kernels, local(): pl.pallas_call(chunk_kernel, out_shape=(shape((2, dk, 2 * dk), BF16), sha...  4.85 us
    ppermute x4, starting transfers between devices, over_chips(): return lax.ppermute(array, 'context', pairs)  2.67 us
    ppermute x2, starting transfers between devices, within_chip(): return lax.ppermute(array, 'context', pairs)  2.59 us
    pallas_call x1, Pallas kernels, local(): pl.pallas_call(stage_kernel, out_shape=shape(proj_qkvz.shape, BF16), in_s...  1.93 us
    ppermute x1, starting transfers between devices, shifted(): lax.ppermute(array, 'context', [(i, i + by) for i in range(peers - by)])  1.91 us
  transfers between devices with their start and end apart: 7, of which 3 were waited for; matrix products, arithmetic and copies ran while one was open for 0% of the time, Pallas kernels for 3%

profile of v4, /device:TPU:32, one launch (start us, length us, event | category | flops | bytes accessed | tf_op | source)
XLA Modules:
  0.0 95.0 jit_solution(1240114113385648874)
XLA Ops:
  0.0 1.9 %collective-permute-start = (bf16[256,128]{1,0:T(8,128)(2,1)}, bf16[256,128]{1,0:T(8,128)(2,1)S(1)}, u32[]{:S(2)}, u32[]{:S(2)}) collective-permute-start(bf16[256,128]{1,0:T(8,128)(2,1)} %x_ref.1), channel_id=1, source_target_pairs={{0,1},{1,2},{2,3},{3,4},{4,5},{5,6},{6,7},{7,8},{8,9},{9,10},{10,1... | collective-permute-start | bytes 196616 | tf_op jit(solution)/shard_map/ppermute | solution.py:253
  1.9 1.9 %shard_map.92.w_ref = bf16[2048,768]{1,0:T(8,128)(2,1)S(1)} custom-call(bf16[2048,768]{1,0:T(8,128)(2,1)} %w_ref.2), custom_call_target="tpu_custom_call" | custom-call | tf_op jit(solution)/shard_map/pallas_call | solution.py:293
  3.9 0.0 copy-start.2
  3.9 0.0 copy-start.3
  3.9 0.0 copy-start.5
  3.9 0.0 copy-start.6
  3.9 0.0 copy-start.7
  3.9 1.9 %collective-permute-done.rim_ref = bf16[256,128]{1,0:T(8,128)(2,1)S(1)} collective-permute-done((bf16[256,128]{1,0:T(8,128)(2,1)}, bf16[256,128]{1,0:T(8,128)(2,1)S(1)}, u32[]{:S(2)}, u32[]{:S(2)}) %collective-permute-start) | collective-permute-done | bytes 65568 | tf_op jit(solution)/shard_map/ppermute | solution.py:253
  5.8 0.1 shard_map.91
  5.9 0.0 copy-start.4
  5.9 25.1 %all_to_all.10.x_ref = bf16[16,272,128]{2,1,0:T(8,128)(2,1)S(1)} all-to-all(bf16[16,272,128]{2,1,0:T(8,128)(2,1)S(1)} %shard_map.91), channel_id=1, replica_groups=mesh['tensor'=16,'context'=32] {'tensor'}, dimensions={0} | all-to-all | bytes 2228224 | tf_op jit(solution)/shard_map/all_to_all | solution.py:302
  31.0 4.9 %shard_map.93 = (bf16[2,128,256]{2,1,0:T(8,128)(2,1)S(1)}, bf16[2,256,256]{2,1,0:T(8,128)(2,1)S(1)}, f32[2,256,256]{2,1,0:T(8,128)S(1)}, bf16[256,128]{1,0:T(8,1...) custom-call(s32[8]{0:T(128)S(1)} %copy-done.5, s32[1]{0:T(128)} %bitcast.first_ref, ...), custom_call_target="tpu_custom_call" | custom-call | tf_op jit(solution)/shard_map/pallas_call | solution.py:304
  35.9 1.3 %collective-permute-start.1 = (bf16[2,128,256]{2,1,0:T(8,128)(2,1)S(1)}, bf16[2,128,256]{2,1,0:T(8,128)(2,1)S(1)}, u32[]{:S(2)}, u32[]{:S(2)}) collective-permute-start(bf16[2,128,256]{2,1,0:T(8,128)(2,1)S(1)} %get-tuple-element.24.late_ref), channel_id=1, source_target_pairs={{0,1},{2,3},{4,5},{6,7},{8,9},{10,11},{12,13},{14,15},{16,17},{18,... | collective-permute-start | bytes 393224 | tf_op jit(solution)/shard_map/ppermute | solution.py:259
  37.2 0.0 copy-start
  37.2 0.7 shard_map.94
  37.9 0.3 collective-permute-done.1.early_ref.first_half_ref
  38.2 0.2 shard_map.95
  38.4 0.7 collective-permute-start.3
  39.0 0.7 collective-permute-start.2
  39.7 0.0 collective-permute-done.3.early_ref
  39.7 0.2 shard_map.96.late_ref
  39.9 0.7 collective-permute-start.4
  40.6 0.0 collective-permute-done.4.early_ref
  40.6 0.2 shard_map.97.near_ref
  40.8 0.7 collective-permute-start.5
  41.5 0.0 collective-permute-done.5.far_ref
  41.5 0.2 shard_map.98.made_ref
  41.6 1.3 %collective-permute-start.6 = (bf16[2,128,128]{2,1,0:T(8,128)(2,1)S(1)}, bf16[2,128,128]{2,1,0:T(8,128)(2,1)S(1)}, u32[]{:S(2)}, u32[]{:S(2)}) collective-permute-start(bf16[2,128,128]{2,1,0:T(8,128)(2,1)S(1)} %shard_map.98.made_ref), channel_id=1, source_target_pairs={{1,0},{3,2},{5,4},{7,6},{9,8},{11,10},{13,12},{15,14},{17,16},{19,... | collective-permute-start | bytes 196616 | tf_op jit(solution)/shard_map/ppermute | solution.py:259
  42.9 29.8 %collective-permute-done.6.given_ref = bf16[2,128,128]{2,1,0:T(8,128)(2,1)S(1)} collective-permute-done((bf16[2,128,128]{2,1,0:T(8,128)(2,1)S(1)}, bf16[2,128,128]{2,1,0:T(8,128)(2,1)S(1)}, u32[]{:S(2)}, u32[]{:S(2)}) %collective-permute-start.6) | collective-permute-done | bytes 65568 | tf_op jit(solution)/shard_map/ppermute | solution.py:259
  72.8 0.8 shard_map.99
  73.6 20.6 %all_to_all.11 = bf16[16,256,128]{2,1,0:T(8,128)(2,1)S(1)} all-to-all(bf16[16,256,128]{2,1,0:T(8,128)(2,1)S(1)} %shard_map.99), channel_id=1, replica_groups=mesh['tensor'=16,'context'=32] {'tensor'}, dimensions={0} | all-to-all | bytes 2097152 | tf_op jit(solution)/shard_map/all_to_all | solution.py:368
  94.2 0.8 reduce_sum.12
  (11 shorter events, 0.0 us)
Async XLA Ops:
  0.0 5.8 %collective-permute-start = (bf16[256,128]{1,0:T(8,128)(2,1)}, bf16[256,128]{1,0:T(8,128)(2,1)S(1)}, u32[]{:S(2)}, u32[]{:S(2)}) collective-permute-start(bf16[256,128]{1,0:T(8,128)(2,1)} %x_ref.1), channel_id=1, source_target_pairs={{0,1},{1,2},{2,3},{3,4},{4,5},{5,6},{6,7},{7,8},{8,9},{9,10},{10,1... | collective-permute-start | bytes 196616 | tf_op jit(solution)/shard_map/ppermute | solution.py:253
  1.9 3.9 %copy-start.1 = (bf16[256,128]{1,0:T(8,128)(2,1)S(1)}, bf16[256,128]{1,0:T(8,128)(2,1)}, u32[]{:S(2)}) copy-start(bf16[256,128]{1,0:T(8,128)(2,1)} %x_ref.1) | copy-start | bytes 196612
  3.9 27.2 %copy-start.2 = (bf16[2048,4]{0,1:T(4,128)(2,1)S(1)}, bf16[2048,4]{0,1:T(4,128)(2,1)}, u32[]{:S(2)}) copy-start(bf16[2048,4]{0,1:T(4,128)(2,1)} %param.11) | copy-start | bytes 49156
  3.9 27.1 %copy-start.3 = (f32[4,1,512]{2,1,0:T(1,128)S(1)}, f32[4,1,512]{2,1,0:T(1,128)}, u32[]{:S(2)}) copy-start(f32[4,1,512]{2,1,0:T(1,128)} %cw_ref.1) | copy-start | bytes 24580
  3.9 27.1 %copy-start.5 = (s32[8]{0:T(128)S(1)}, s32[8]{0:T(128)}, u32[]{:S(2)}) copy-start(s32[8]{0:T(128)} %lens_ref.1) | copy-start | bytes 100
  3.9 27.1 %copy-start.6 = (f32[2]{0:T(128)S(1)}, f32[2]{0:T(128)}, u32[]{:S(2)}) copy-start(f32[2]{0:T(128)} %rate_ref.1) | copy-start | bytes 28
  3.9 27.1 %copy-start.7 = (f32[2]{0:T(128)S(1)}, f32[2]{0:T(128)}, u32[]{:S(2)}) copy-start(f32[2]{0:T(128)} %bias_ref.1) | copy-start | bytes 28
  5.9 31.3 %copy-start.4 = (f32[128]{0:T(128)S(1)}, f32[128]{0:T(128)}, u32[]{:S(2)}) copy-start(f32[128]{0:T(128)} %param.15) | copy-start | bytes 1540
  35.9 2.3 %collective-permute-start.1 = (bf16[2,128,256]{2,1,0:T(8,128)(2,1)S(1)}, bf16[2,128,256]{2,1,0:T(8,128)(2,1)S(1)}, u32[]{:S(2)}, u32[]{:S(2)}) collective-permute-start(bf16[2,128,256]{2,1,0:T(8,128)(2,1)S(1)} %get-tuple-element.24.late_ref), channel_id=1, source_target_pairs={{0,1},{2,3},{4,5},{6,7},{8,9},{10,11},{12,13},{14,15},{16,17},{18,... | collective-permute-start | bytes 393224 | tf_op jit(solution)/shard_map/ppermute | solution.py:259
  37.2 35.6 %copy-start = (bf16[256,2048]{1,0:T(8,128)(2,1)S(1)}, bf16[256,2048]{1,0:T(8,128)(2,1)}, u32[]{:S(2)}) copy-start(bf16[256,2048]{1,0:T(8,128)(2,1)} %w_ref.3) | copy-start | bytes 3145732
  38.4 1.4 %collective-permute-start.3 = (bf16[2,128,256]{2,1,0:T(8,128)(2,1)S(1)}, bf16[2,128,256]{2,1,0:T(8,128)(2,1)S(1)}, u32[]{:S(2)}, u32[]{:S(2)}) collective-permute-start(bf16[2,128,256]{2,1,0:T(8,128)(2,1)S(1)} %shard_map.95), channel_id=1, source_target_pairs={{1,5},{3,7},{5,9},{7,11},{9,13},{11,15},{13,17},{15,19},{17,21},{1... | collective-permute-start | bytes 393224 | tf_op jit(solution)/shard_map/ppermute | solution.py:265
  39.0 0.7 collective-permute-start.2
  39.9 0.7 collective-permute-start.4
  40.8 0.7 collective-permute-start.5
  41.6 31.1 %collective-permute-start.6 = (bf16[2,128,128]{2,1,0:T(8,128)(2,1)S(1)}, bf16[2,128,128]{2,1,0:T(8,128)(2,1)S(1)}, u32[]{:S(2)}, u32[]{:S(2)}) collective-permute-start(bf16[2,128,128]{2,1,0:T(8,128)(2,1)S(1)} %shard_map.98.made_ref), channel_id=1, source_target_pairs={{1,0},{3,2},{5,4},{7,6},{9,8},{11,10},{13,12},{15,14},{17,16},{19,... | collective-permute-start | bytes 196616 | tf_op jit(solution)/shard_map/ppermute | solution.py:259

commit v5 on v4

--- a/solution.py
+++ b/solution.py
@@ -236,6 +236,13 @@
         out_ref[part] = share[:, part * width : (part + 1) * width]
 
 
+def sum_kernel(shares_ref, out_ref):
+    total = shares_ref[0].astype(F32)
+    for part in range(1, shares_ref.shape[0]):
+        total = total + shares_ref[part].astype(F32)
+    out_ref[...] = total.astype(BF16)
+
+
 def vmem():
     return pl.BlockSpec(memory_space=pltpu.VMEM)
 
@@ -366,7 +373,13 @@
         compiler_params=params(),
     )(made, given, first_half, follow, own, gate, proj_out)
     shares = lax.all_to_all(share, "tensor", 0, 0, tiled=True)
-    return jnp.sum(shares.astype(F32), axis=0).astype(BF16)
+    return pl.pallas_call(
+        sum_kernel,
+        out_shape=shape((rows, width), BF16),
+        in_specs=[vmem()],
+        out_specs=vmem(),
+        compiler_params=params(),
+    )(shares)
 
 
 def solution(mesh):

time: 95.3 us -> 95.3 us (level)
  no operation moved by 1% of the time
where the time goes in v5:
time: 95.3 us; the launch traced here: 95 us
  blocking collectives  45.7 us (48%)
  waiting for transfers between devices  32 us (34%)
  Pallas kernels  9.81 us (10%)
  starting transfers between devices  7.17 us (8%)
    ppermute x2, waiting for transfers between devices, within_chip(): return lax.ppermute(array, 'context', pairs)  30.1 us
    all_to_all x1, blocking collectives, local(): gathered = lax.all_to_all(spread, 'tensor', 0, 0, tiled=True)  25.1 us
    all_to_all x1, blocking collectives, local(): shares = lax.all_to_all(share, 'tensor', 0, 0, tiled=True)  20.6 us
    pallas_call x1, Pallas kernels, local(): pl.pallas_call(chunk_kernel, out_shape=(shape((2, dk, 2 * dk), BF16), sha...  4.85 us
    ppermute x4, starting transfers between devices, over_chips(): return lax.ppermute(array, 'context', pairs)  2.67 us
    ppermute x2, starting transfers between devices, within_chip(): return lax.ppermute(array, 'context', pairs)  2.59 us
    pallas_call x1, Pallas kernels, local(): pl.pallas_call(stage_kernel, out_shape=shape(proj_qkvz.shape, BF16), in_s...  1.93 us
    ppermute x1, starting transfers between devices, shifted(): lax.ppermute(array, 'context', [(i, i + by) for i in range(peers - by)])  1.91 us
  transfers between devices with their start and end apart: 7, of which 3 were waited for; matrix products, arithmetic and copies ran while one was open for 0% of the time, Pallas kernels for 3%

profile of v5, /device:TPU:32, one launch (start us, length us, event | category | flops | bytes accessed | tf_op | source)
XLA Modules:
  0.0 95.0 jit_solution(4847118658853499464)
XLA Ops:
  0.0 1.9 %collective-permute-start = (bf16[256,128]{1,0:T(8,128)(2,1)}, bf16[256,128]{1,0:T(8,128)(2,1)S(1)}, u32[]{:S(2)}, u32[]{:S(2)}) collective-permute-start(bf16[256,128]{1,0:T(8,128)(2,1)} %x_ref.1), channel_id=1, source_target_pairs={{0,1},{1,2},{2,3},{3,4},{4,5},{5,6},{6,7},{7,8},{8,9},{9,10},{10,1... | collective-permute-start | bytes 196616 | tf_op jit(solution)/shard_map/ppermute | solution.py:260
  1.9 1.9 %shard_map.92.w_ref = bf16[2048,768]{1,0:T(8,128)(2,1)S(1)} custom-call(bf16[2048,768]{1,0:T(8,128)(2,1)} %w_ref.2), custom_call_target="tpu_custom_call" | custom-call | tf_op jit(solution)/shard_map/pallas_call | solution.py:300
  3.9 0.0 copy-start.2
  3.9 0.0 copy-start.3
  3.9 0.0 copy-start.5
  3.9 0.0 copy-start.6
  3.9 0.0 copy-start.7
  3.9 1.9 %collective-permute-done.rim_ref = bf16[256,128]{1,0:T(8,128)(2,1)S(1)} collective-permute-done((bf16[256,128]{1,0:T(8,128)(2,1)}, bf16[256,128]{1,0:T(8,128)(2,1)S(1)}, u32[]{:S(2)}, u32[]{:S(2)}) %collective-permute-start) | collective-permute-done | bytes 65568 | tf_op jit(solution)/shard_map/ppermute | solution.py:260
  5.8 0.1 shard_map.91
  5.9 0.0 copy-start.4
  5.9 25.1 %all_to_all.10.x_ref = bf16[16,272,128]{2,1,0:T(8,128)(2,1)S(1)} all-to-all(bf16[16,272,128]{2,1,0:T(8,128)(2,1)S(1)} %shard_map.91), channel_id=1, replica_groups=mesh['tensor'=16,'context'=32] {'tensor'}, dimensions={0} | all-to-all | bytes 2228224 | tf_op jit(solution)/shard_map/all_to_all | solution.py:309
  31.0 4.9 %shard_map.93 = (bf16[2,128,256]{2,1,0:T(8,128)(2,1)S(1)}, bf16[2,256,256]{2,1,0:T(8,128)(2,1)S(1)}, f32[2,256,256]{2,1,0:T(8,128)S(1)}, bf16[256,128]{1,0:T(8,1...) custom-call(s32[8]{0:T(128)S(1)} %copy-done.5, s32[1]{0:T(128)} %bitcast.first_ref, ...), custom_call_target="tpu_custom_call" | custom-call | tf_op jit(solution)/shard_map/pallas_call | solution.py:311
  35.9 1.3 %collective-permute-start.1 = (bf16[2,128,256]{2,1,0:T(8,128)(2,1)S(1)}, bf16[2,128,256]{2,1,0:T(8,128)(2,1)S(1)}, u32[]{:S(2)}, u32[]{:S(2)}) collective-permute-start(bf16[2,128,256]{2,1,0:T(8,128)(2,1)S(1)} %get-tuple-element.24.late_ref), channel_id=1, source_target_pairs={{0,1},{2,3},{4,5},{6,7},{8,9},{10,11},{12,13},{14,15},{16,17},{18,... | collective-permute-start | bytes 393224 | tf_op jit(solution)/shard_map/ppermute | solution.py:266
  37.2 0.0 copy-start
  37.2 0.7 shard_map.94
  37.9 0.3 collective-permute-done.1.early_ref.first_half_ref
  38.2 0.2 shard_map.95
  38.4 0.7 collective-permute-start.3
  39.0 0.7 collective-permute-start.2
  39.7 0.0 collective-permute-done.3.early_ref
  39.7 0.2 shard_map.96.late_ref
  39.9 0.7 collective-permute-start.4
  40.6 0.0 collective-permute-done.4.early_ref
  40.6 0.2 shard_map.97.near_ref
  40.8 0.7 collective-permute-start.5
  41.5 0.0 collective-permute-done.5.far_ref
  41.5 0.2 shard_map.98.made_ref
  41.6 1.3 %collective-permute-start.6 = (bf16[2,128,128]{2,1,0:T(8,128)(2,1)S(1)}, bf16[2,128,128]{2,1,0:T(8,128)(2,1)S(1)}, u32[]{:S(2)}, u32[]{:S(2)}) collective-permute-start(bf16[2,128,128]{2,1,0:T(8,128)(2,1)S(1)} %shard_map.98.made_ref), channel_id=1, source_target_pairs={{1,0},{3,2},{5,4},{7,6},{9,8},{11,10},{13,12},{15,14},{17,16},{19,... | collective-permute-start | bytes 196616 | tf_op jit(solution)/shard_map/ppermute | solution.py:266
  42.9 29.8 %collective-permute-done.6.given_ref = bf16[2,128,128]{2,1,0:T(8,128)(2,1)S(1)} collective-permute-done((bf16[2,128,128]{2,1,0:T(8,128)(2,1)S(1)}, bf16[2,128,128]{2,1,0:T(8,128)(2,1)S(1)}, u32[]{:S(2)}, u32[]{:S(2)}) %collective-permute-start.6) | collective-permute-done | bytes 65568 | tf_op jit(solution)/shard_map/ppermute | solution.py:266
  72.8 0.8 shard_map.99
  73.6 20.6 %all_to_all.11.shares_ref = bf16[16,256,128]{2,1,0:T(8,128)(2,1)S(1)} all-to-all(bf16[16,256,128]{2,1,0:T(8,128)(2,1)S(1)} %shard_map.99), channel_id=1, replica_groups=mesh['tensor'=16,'context'=32] {'tensor'}, dimensions={0} | all-to-all | bytes 2097152 | tf_op jit(solution)/shard_map/all_to_all | solution.py:375
  94.2 0.8 shard_map.100
  (11 shorter events, 0.0 us)
Async XLA Ops:
  0.0 5.8 %collective-permute-start = (bf16[256,128]{1,0:T(8,128)(2,1)}, bf16[256,128]{1,0:T(8,128)(2,1)S(1)}, u32[]{:S(2)}, u32[]{:S(2)}) collective-permute-start(bf16[256,128]{1,0:T(8,128)(2,1)} %x_ref.1), channel_id=1, source_target_pairs={{0,1},{1,2},{2,3},{3,4},{4,5},{5,6},{6,7},{7,8},{8,9},{9,10},{10,1... | collective-permute-start | bytes 196616 | tf_op jit(solution)/shard_map/ppermute | solution.py:260
  1.9 3.9 %copy-start.1 = (bf16[256,128]{1,0:T(8,128)(2,1)S(1)}, bf16[256,128]{1,0:T(8,128)(2,1)}, u32[]{:S(2)}) copy-start(bf16[256,128]{1,0:T(8,128)(2,1)} %x_ref.1) | copy-start | bytes 196612
  3.9 27.2 %copy-start.2 = (bf16[2048,4]{0,1:T(4,128)(2,1)S(1)}, bf16[2048,4]{0,1:T(4,128)(2,1)}, u32[]{:S(2)}) copy-start(bf16[2048,4]{0,1:T(4,128)(2,1)} %param.11) | copy-start | bytes 49156
  3.9 27.1 %copy-start.3 = (f32[4,1,512]{2,1,0:T(1,128)S(1)}, f32[4,1,512]{2,1,0:T(1,128)}, u32[]{:S(2)}) copy-start(f32[4,1,512]{2,1,0:T(1,128)} %cw_ref.1) | copy-start | bytes 24580
  3.9 27.1 %copy-start.5 = (s32[8]{0:T(128)S(1)}, s32[8]{0:T(128)}, u32[]{:S(2)}) copy-start(s32[8]{0:T(128)} %lens_ref.1) | copy-start | bytes 100
  3.9 27.1 %copy-start.6 = (f32[2]{0:T(128)S(1)}, f32[2]{0:T(128)}, u32[]{:S(2)}) copy-start(f32[2]{0:T(128)} %rate_ref.1) | copy-start | bytes 28
  3.9 27.1 %copy-start.7 = (f32[2]{0:T(128)S(1)}, f32[2]{0:T(128)}, u32[]{:S(2)}) copy-start(f32[2]{0:T(128)} %bias_ref.1) | copy-start | bytes 28
  5.9 31.3 %copy-start.4 = (f32[128]{0:T(128)S(1)}, f32[128]{0:T(128)}, u32[]{:S(2)}) copy-start(f32[128]{0:T(128)} %param.15) | copy-start | bytes 1540
  35.9 2.3 %collective-permute-start.1 = (bf16[2,128,256]{2,1,0:T(8,128)(2,1)S(1)}, bf16[2,128,256]{2,1,0:T(8,128)(2,1)S(1)}, u32[]{:S(2)}, u32[]{:S(2)}) collective-permute-start(bf16[2,128,256]{2,1,0:T(8,128)(2,1)S(1)} %get-tuple-element.24.late_ref), channel_id=1, source_target_pairs={{0,1},{2,3},{4,5},{6,7},{8,9},{10,11},{12,13},{14,15},{16,17},{18,... | collective-permute-start | bytes 393224 | tf_op jit(solution)/shard_map/ppermute | solution.py:266
  37.2 35.6 %copy-start = (bf16[256,2048]{1,0:T(8,128)(2,1)S(1)}, bf16[256,2048]{1,0:T(8,128)(2,1)}, u32[]{:S(2)}) copy-start(bf16[256,2048]{1,0:T(8,128)(2,1)} %w_ref.3) | copy-start | bytes 3145732
  38.4 1.4 %collective-permute-start.3 = (bf16[2,128,256]{2,1,0:T(8,128)(2,1)S(1)}, bf16[2,128,256]{2,1,0:T(8,128)(2,1)S(1)}, u32[]{:S(2)}, u32[]{:S(2)}) collective-permute-start(bf16[2,128,256]{2,1,0:T(8,128)(2,1)S(1)} %shard_map.95), channel_id=1, source_target_pairs={{1,5},{3,7},{5,9},{7,11},{9,13},{11,15},{13,17},{15,19},{17,21},{1... | collective-permute-start | bytes 393224 | tf_op jit(solution)/shard_map/ppermute | solution.py:272
  39.0 0.7 collective-permute-start.2
  39.9 0.7 collective-permute-start.4
  40.8 0.7 collective-permute-start.5
  41.6 31.1 %collective-permute-start.6 = (bf16[2,128,128]{2,1,0:T(8,128)(2,1)S(1)}, bf16[2,128,128]{2,1,0:T(8,128)(2,1)S(1)}, u32[]{:S(2)}, u32[]{:S(2)}) collective-permute-start(bf16[2,128,128]{2,1,0:T(8,128)(2,1)S(1)} %shard_map.98.made_ref), channel_id=1, source_target_pairs={{1,0},{3,2},{5,4},{7,6},{9,8},{11,10},{13,12},{15,14},{17,16},{19,... | collective-permute-start | bytes 196616 | tf_op jit(solution)/shard_map/ppermute | solution.py:266
